TPU v7x, 32 devices: a whole 2x2x4 slice. The times are simulated.
32 devices in a mesh: seq: 32 (over z, y, x, core).
Axes of the slice: x: 2, y: 2, z: 4, core: 2. Of those that a mesh axis runs over, the one named last changes fastest.
Arguments:
- inputs: bfloat16 [16384, 768], P('seq'), may hold values from -6 to 6
- segment_ids: int32 [32, 512], P('seq'), may hold values from 0 to 3, never falling along the last dimension, each value on 1 to 256 neighbouring positions
- routes: int32 [16384, 1], P('seq'), may hold values from 0 to 31
- cotangent: bfloat16 [16384, 768], P('seq'), may hold values from -6 to 6
- gain_attn: float32 [768], P('seq'), may hold values from 0.1 to 1.9
- gain_ffn: float32 [768], P('seq'), may hold values from 0.1 to 1.9
- bias_table: float32 [384], P('seq'), may hold values from -4 to 4
- w_query: float32 [768, 768], P('seq'), may hold values from -0.21875 to 0.21875
- w_key: float32 [768, 768], P('seq'), may hold values from -0.21875 to 0.21875
- w_value: float32 [768, 768], P('seq'), may hold values from -0.21875 to 0.21875
- w_output: float32 [768, 768], P('seq'), may hold values from -2.5 to 2.5
- w_router: float32 [768, 32], P('seq'), may hold values from -0.108 to 0.108
- w_in: float32 [32, 768, 3072], P('seq'), may hold values from -0.21875 to 0.21875
- w_out: float32 [32, 3072, 768], P('seq'), may hold values from -3.4641016 to 3.4641016
Outputs:
- outputs: bfloat16 [16384, 768], P('seq')
- grad_inputs: bfloat16 [16384, 768], P('seq')
- grad_gain_attn: float32 [768], P('seq')
- grad_gain_ffn: float32 [768], P('seq')
- grad_bias_table: float32 [384], P('seq')
- grad_w_query: float32 [768, 768], P('seq')
- grad_w_key: float32 [768, 768], P('seq')
- grad_w_value: float32 [768, 768], P('seq')
- grad_w_output: float32 [768, 768], P('seq')
- grad_w_router: float32 [768, 32], P('seq')
- grad_w_in: float32 [32, 768, 3072], P('seq')
- grad_w_out: float32 [32, 3072, 768], P('seq')
Inputs may be any that keep to these rules, and one draw needn't show every extreme that they name: `segment_ids`: along each packed row of 512 positions the ids never fall.
All inputs are finite; a program needn't handle non-finite values.
Results may differ from a plain program's by a relative error of at most 0.017.
The roundings to bfloat16 on the way count: a program that leaves them out, or rounds other values in their place, can miss the bound.
Values may be sent and summed in bfloat16 or wider, within the bound.
No kernel may reach another device: no remote copies, remote signals or barrier semaphores. Data moves between devices by JAX's collectives and lax.ppermute only.
A program may use at most 256 MiB of HBM per device.

v0:
```python
import jax
import jax.numpy as jnp
from jax import lax
from jax.sharding import PartitionSpec as P

HEADS = 12
HEAD_DIM = 64
BUCKETS = 32


epsilon = 1e-06
bucket_edges = (1, 2, 3, 4, 5, 6, 7, 8, 12, 16, 23, 32, 46, 64, 91)
gelu_coef = 0.7978845608028654
cubic_coef = 0.044715


def gelu_tanh(values):
    return (
        0.5
        * values
        * (1.0 + jnp.tanh(gelu_coef * (values + cubic_coef * values * values * values)))
    )


def gelu_slope(values):
    squared = values * values
    bent = jnp.tanh(gelu_coef * (values + cubic_coef * squared * values))
    return 0.5 * (1.0 + bent) + 0.5 * values * (1.0 - bent * bent) * gelu_coef * (
        1.0 + 3.0 * cubic_coef * squared
    )


def relative_onehot(length):
    offset = lax.broadcasted_iota(jnp.int32, (length, length), 1) - lax.broadcasted_iota(
        jnp.int32, (length, length), 0
    )
    magnitude = jnp.abs(offset)
    bucket = jnp.zeros((length, length), jnp.int32)
    for edge_value in bucket_edges:
        bucket = bucket + (magnitude >= edge_value).astype(jnp.int32)
    bucket = bucket + BUCKETS // 2 * (offset > 0).astype(jnp.int32)
    labels = lax.broadcasted_iota(jnp.int32, (BUCKETS, length, length), 0)
    return (labels == bucket[None]).astype(jnp.bfloat16).reshape(BUCKETS, length * length)


def make_bias(table, onehot, length):
    flat_bias = lax.dot_general(
        table.reshape(BUCKETS, HEADS),
        onehot,
        (((0,), (0,)), ((), ())),
        preferred_element_type=jnp.float32,
    )
    return flat_bias.reshape(HEADS, length, length)


def norm_forward(values, gain_vec):
    inverse = lax.rsqrt(jnp.mean(values * values, axis=-1, keepdims=True) + epsilon)
    unit_rows = values * inverse
    return (unit_rows * gain_vec, unit_rows, inverse)


def norm_backward(unit_rows, inverse, gain_vec, grad_in):
    scaled = grad_in * gain_vec
    grad_back = inverse * (
        scaled - unit_rows * jnp.mean(scaled * unit_rows, axis=-1, keepdims=True)
    )
    return (grad_back, jnp.sum(grad_in * unit_rows, axis=0))


def head_scores(query_rows, key_rows, segments, score_bias, score_scale):
    length = query_rows.shape[0]
    query_heads = query_rows.reshape(length, HEADS, HEAD_DIM)
    key_heads = key_rows.reshape(length, HEADS, HEAD_DIM)
    scores = (
        jnp.einsum("qhd,khd->hqk", query_heads, key_heads, preferred_element_type=jnp.float32)
        * score_scale
        + score_bias
    )
    same_doc = segments[:, None] == segments[None, :]
    return jnp.where(same_doc[None], scores, -1000000000.0)


def attend_forward(query_rows, key_rows, value_rows, segments, score_bias, score_scale):
    length = query_rows.shape[0]
    scores = head_scores(query_rows, key_rows, segments, score_bias, score_scale)
    row_max = jnp.max(scores, axis=-1, keepdims=True)
    weights = jnp.exp(scores - row_max)
    row_total = jnp.sum(weights, axis=-1, keepdims=True)
    attn_probs = (weights / row_total).astype(jnp.bfloat16)
    value_heads = value_rows.reshape(length, HEADS, HEAD_DIM)
    mixed_heads = jnp.einsum(
        "hqk,khd->qhd", attn_probs, value_heads, preferred_element_type=jnp.float32
    )
    return (
        mixed_heads.reshape(length, HEADS * HEAD_DIM).astype(jnp.bfloat16),
        (row_max + jnp.log(row_total))[:, :, 0],
    )


def attend_backward(
    query_rows, key_rows, value_rows, grad_mixed, segments, logsum, score_bias, onehot, score_scale
):
    length = query_rows.shape[0]
    scores = head_scores(query_rows, key_rows, segments, score_bias, score_scale)
    attn_probs = jnp.exp(scores - logsum[:, :, None])
    query_heads = query_rows.reshape(length, HEADS, HEAD_DIM)
    key_heads = key_rows.reshape(length, HEADS, HEAD_DIM)
    value_heads = value_rows.reshape(length, HEADS, HEAD_DIM)
    grad_heads = grad_mixed.reshape(length, HEADS, HEAD_DIM)
    grad_probs = jnp.einsum(
        "qhd,khd->hqk", grad_heads, value_heads, preferred_element_type=jnp.float32
    )
    grad_value = jnp.einsum(
        "hqk,qhd->khd",
        attn_probs.astype(jnp.bfloat16),
        grad_heads,
        preferred_element_type=jnp.float32,
    )
    inner_sum = jnp.sum(attn_probs * grad_probs, axis=-1, keepdims=True)
    grad_scores = (attn_probs * (grad_probs - inner_sum)).astype(jnp.bfloat16)
    grad_query = (
        jnp.einsum("hqk,khd->qhd", grad_scores, key_heads, preferred_element_type=jnp.float32)
        * score_scale
    )
    grad_key = (
        jnp.einsum("hqk,qhd->khd", grad_scores, query_heads, preferred_element_type=jnp.float32)
        * score_scale
    )
    grad_table = lax.dot_general(
        onehot,
        grad_scores.reshape(HEADS, length * length),
        (((1,), (1,)), ((), ())),
        preferred_element_type=jnp.float32,
    )
    flat = HEADS * HEAD_DIM
    return (
        grad_query.reshape(length, flat).astype(jnp.bfloat16),
        grad_key.reshape(length, flat).astype(jnp.bfloat16),
        grad_value.reshape(length, flat).astype(jnp.bfloat16),
        grad_table,
    )


def rows_product(left, right):
    return lax.dot_general(
        left, right, (((0,), (0,)), ((), ())), preferred_element_type=jnp.float32
    )


def back_product(left, right):
    return lax.dot_general(
        left, right, (((1,), (1,)), ((), ())), preferred_element_type=jnp.float32
    )


def shards(
    inputs,
    segment_ids,
    routes,
    cotangent,
    gain_attn,
    gain_ffn,
    bias_table,
    w_query,
    w_key,
    w_value,
    w_output,
    w_router,
    w_in,
    w_out,
):
    devices = lax.axis_size("seq")
    tokens = inputs.shape[0]
    model_width = inputs.shape[1]
    sequences = segment_ids.shape[0]
    length = segment_ids.shape[1]
    experts = w_router.shape[1]
    local_experts = w_in.shape[0]
    capacity = max(2, 5 * tokens // (4 * experts))
    score_scale = HEAD_DIM ** (-0.5)
    slot_count = experts * capacity
    fetched = (
        lax.all_gather(gain_attn.astype(jnp.bfloat16), "seq", axis=0, tiled=True),
        lax.all_gather(gain_ffn.astype(jnp.bfloat16), "seq", axis=0, tiled=True),
        lax.all_gather(bias_table.astype(jnp.bfloat16), "seq", axis=0, tiled=True),
        lax.all_gather(w_query.astype(jnp.bfloat16), "seq", axis=0, tiled=True),
        lax.all_gather(w_key.astype(jnp.bfloat16), "seq", axis=0, tiled=True),
        lax.all_gather(w_value.astype(jnp.bfloat16), "seq", axis=0, tiled=True),
        lax.all_gather(w_output.astype(jnp.bfloat16), "seq", axis=0, tiled=True),
        lax.all_gather(w_router.astype(jnp.bfloat16), "seq", axis=0, tiled=True),
    )
    gain_one, gain_two, table, query_w, key_w, value_w, output_w, router_w = fetched
    onehot = relative_onehot(length)
    score_bias = make_bias(table, onehot, length)
    first_input = inputs.astype(jnp.float32)
    normed_one, unit_one, inverse_one = norm_forward(first_input, gain_one.astype(jnp.float32))
    low_one = normed_one.astype(jnp.bfloat16)
    query = jnp.dot(low_one, query_w, preferred_element_type=jnp.float32).astype(jnp.bfloat16)
    key_rows = jnp.dot(low_one, key_w, preferred_element_type=jnp.float32).astype(jnp.bfloat16)
    value_rows = jnp.dot(low_one, value_w, preferred_element_type=jnp.float32).astype(jnp.bfloat16)
    shape_rows = (sequences, length, model_width)
    mixed, logsum = lax.map(
        lambda pieces: attend_forward(
            pieces[0], pieces[1], pieces[2], pieces[3], score_bias, score_scale
        ),
        (
            query.reshape(shape_rows),
            key_rows.reshape(shape_rows),
            value_rows.reshape(shape_rows),
            segment_ids,
        ),
    )
    mixed = mixed.reshape(tokens, model_width)
    after_attn = first_input + jnp.dot(mixed, output_w, preferred_element_type=jnp.float32)
    normed_two, unit_two, inverse_two = norm_forward(after_attn, gain_two.astype(jnp.float32))
    low_two = normed_two.astype(jnp.bfloat16)
    logits = jnp.dot(low_two, router_w, preferred_element_type=jnp.float32)
    router_probs = jax.nn.softmax(logits, axis=-1)
    labels = lax.broadcasted_iota(jnp.int32, (tokens, experts), 1)
    picked = routes == labels
    picked_float = picked.astype(jnp.float32)
    gate_prob = jnp.sum(router_probs * picked_float, axis=1, keepdims=True)
    earlier = (
        lax.broadcasted_iota(jnp.int32, (tokens, tokens), 1)
        <= lax.broadcasted_iota(jnp.int32, (tokens, tokens), 0)
    ).astype(jnp.bfloat16)
    counts = jnp.dot(earlier, picked.astype(jnp.bfloat16), preferred_element_type=jnp.float32)
    position = jnp.sum(counts * picked_float, axis=1) - 1.0
    slot_index = jnp.where(
        position < capacity, routes[:, 0] * capacity + position.astype(jnp.int32), -1
    )
    dispatch = (
        lax.broadcasted_iota(jnp.int32, (slot_count, tokens), 0) == slot_index[None, :]
    ).astype(jnp.bfloat16)
    buffer_shape = (devices, local_experts * capacity, model_width)
    expert_shape = (devices, local_experts, capacity, model_width)
    send_rows = (
        jnp.dot(dispatch, low_two, preferred_element_type=jnp.float32)
        .astype(jnp.bfloat16)
        .reshape(buffer_shape)
    )
    grad_out = cotangent.astype(jnp.float32)
    grad_rows = (gate_prob * grad_out).astype(jnp.bfloat16)
    grad_send = (
        jnp.dot(dispatch, grad_rows, preferred_element_type=jnp.float32)
        .astype(jnp.bfloat16)
        .reshape(buffer_shape)
    )
    received = lax.all_to_all(send_rows, "seq", split_axis=0, concat_axis=0, tiled=True).reshape(
        expert_shape
    )
    inner_low = w_in.astype(jnp.bfloat16)
    outer_low = w_out.astype(jnp.bfloat16)
    pre_act = jnp.einsum("secd,edf->secf", received, inner_low, preferred_element_type=jnp.float32)
    hidden = gelu_tanh(pre_act).astype(jnp.bfloat16)
    produced = jnp.einsum(
        "secf,efd->secd", hidden, outer_low, preferred_element_type=jnp.float32
    ).astype(jnp.bfloat16)
    returned = lax.all_to_all(
        produced.reshape(buffer_shape), "seq", split_axis=0, concat_axis=0, tiled=True
    )
    expert_rows = rows_product(dispatch, returned.reshape(slot_count, model_width))
    output = (after_attn + gate_prob * expert_rows).astype(jnp.bfloat16)
    grad_gate = jnp.sum(grad_out * expert_rows, axis=1, keepdims=True)
    grad_received = lax.all_to_all(
        grad_send, "seq", split_axis=0, concat_axis=0, tiled=True
    ).reshape(expert_shape)
    grad_hidden = jnp.einsum(
        "secd,efd->secf", grad_received, outer_low, preferred_element_type=jnp.float32
    )
    grad_act = (grad_hidden * gelu_slope(pre_act)).astype(jnp.bfloat16)
    grad_outer = jnp.einsum(
        "secf,secd->efd", hidden, grad_received, preferred_element_type=jnp.float32
    )
    grad_inner = jnp.einsum(
        "secd,secf->edf", received, grad_act, preferred_element_type=jnp.float32
    )
    grad_expert_in = jnp.einsum(
        "secf,edf->secd", grad_act, inner_low, preferred_element_type=jnp.float32
    ).astype(jnp.bfloat16)
    grad_back = lax.all_to_all(
        grad_expert_in.reshape(buffer_shape), "seq", split_axis=0, concat_axis=0, tiled=True
    )
    grad_normed_two = rows_product(dispatch, grad_back.reshape(slot_count, model_width))
    grad_logits = (router_probs * (picked_float - gate_prob) * grad_gate).astype(jnp.bfloat16)
    grad_router = rows_product(low_two, grad_logits)
    grad_normed_two = grad_normed_two + back_product(grad_logits, router_w)
    back_two, grad_gain_two = norm_backward(
        unit_two, inverse_two, gain_two.astype(jnp.float32), grad_normed_two
    )
    grad_after = grad_out + back_two
    grad_attn_low = grad_after.astype(jnp.bfloat16)
    grad_output_w = rows_product(mixed, grad_attn_low)
    grad_mixed = back_product(grad_attn_low, output_w).astype(jnp.bfloat16)
    grad_query, grad_key, grad_value, grad_tables = lax.map(
        lambda pieces: attend_backward(
            pieces[0],
            pieces[1],
            pieces[2],
            pieces[3],
            pieces[4],
            pieces[5],
            score_bias,
            onehot,
            score_scale,
        ),
        (
            query.reshape(shape_rows),
            key_rows.reshape(shape_rows),
            value_rows.reshape(shape_rows),
            grad_mixed.reshape(shape_rows),
            segment_ids,
            logsum,
        ),
    )
    grad_table = jnp.sum(grad_tables, axis=0).reshape(BUCKETS * HEADS)
    grad_query = grad_query.reshape(tokens, model_width)
    grad_key = grad_key.reshape(tokens, model_width)
    grad_value = grad_value.reshape(tokens, model_width)
    grad_query_w = rows_product(low_one, grad_query)
    grad_key_w = rows_product(low_one, grad_key)
    grad_value_w = rows_product(low_one, grad_value)
    grad_normed = (
        back_product(grad_query, query_w)
        + back_product(grad_key, key_w)
        + back_product(grad_value, value_w)
    )
    back_one, grad_gain_one = norm_backward(
        unit_one, inverse_one, gain_one.astype(jnp.float32), grad_normed
    )
    grad_inputs = (grad_after + back_one).astype(jnp.bfloat16)
    summed = (
        lax.psum_scatter(grad_gain_one, "seq", scatter_dimension=0, tiled=True),
        lax.psum_scatter(grad_gain_two, "seq", scatter_dimension=0, tiled=True),
        lax.psum_scatter(grad_table, "seq", scatter_dimension=0, tiled=True),
        lax.psum_scatter(grad_query_w, "seq", scatter_dimension=0, tiled=True),
        lax.psum_scatter(grad_key_w, "seq", scatter_dimension=0, tiled=True),
        lax.psum_scatter(grad_value_w, "seq", scatter_dimension=0, tiled=True),
        lax.psum_scatter(grad_output_w, "seq", scatter_dimension=0, tiled=True),
        lax.psum_scatter(grad_router, "seq", scatter_dimension=0, tiled=True),
    )
    return (
        output,
        grad_inputs,
        summed[0],
        summed[1],
        summed[2],
        summed[3],
        summed[4],
        summed[5],
        summed[6],
        summed[7],
        grad_inner,
        grad_outer,
    )


def solution(mesh):
    in_specs = (
        P("seq", None),
        P("seq", None),
        P("seq", None),
        P("seq", None),
        P("seq"),
        P("seq"),
        P("seq"),
        P("seq", None),
        P("seq", None),
        P("seq", None),
        P("seq", None),
        P("seq", None),
        P("seq", None, None),
        P("seq", None, None),
    )
    out_specs = (
        P("seq", None),
        P("seq", None),
        P("seq"),
        P("seq"),
        P("seq"),
        P("seq", None),
        P("seq", None),
        P("seq", None),
        P("seq", None),
        P("seq", None),
        P("seq", None, None),
        P("seq", None, None),
    )
    return jax.shard_map(shards, mesh=mesh, in_specs=in_specs, out_specs=out_specs, check_vma=False)
```

profile of v0, /device:TPU:0, one launch (start us, length us, event | category | flops | bytes accessed | tf_op | source)
XLA Modules:
  0.0 962.7 jit_solution(5186060791678395056)
XLA Ops:
  7.2 1.6 convert_element_type.307
  16.8 42.1 %all-reduce.8 = (bf16[768]{0:T(1024)(128)(2,1)S(1)}, bf16[384]{0:T(512)(128)(2,1)S(1)}, bf16[768]{0:T(1024)(128)(2,1)S(1)}) all-reduce(bf16[768]{0:T(1024)(128)(2,1)S(1)} %dynamic-update-slice, bf16[384]{0:T(512)(128)(2,1)S(1)} %dynamic-update-slice.1, bf16[768]{0:T(1024)(128)(2,1)S(1)} %dynamic-update-slice.2), channel_id=1, replica_groups=mesh['seq'=32] {'seq'}, use_global_device_ids=true, to_apply=%add | all-reduce | flops 1920 | bytes 7680
  59.2 8.1 iota_compare_fusion
  67.3 9.6 copy.83
  76.9 7.6 fusion.123
  84.5 18.0 %copy.84 = f32[2,8,512,512]{3,2,1,0:T(8,128)} copy(f32[2,8,512,512]{3,1,2,0:T(8,128)} %bitcast.141) | data formatting | bytes 33554432
  102.5 10.6 %slice = f32[12,512,512]{2,1,0:T(8,128)} slice(f32[16,512,512]{2,1,0:T(8,128)} %bitcast.143), slice={[0:12], [0:512], [0:512]} | slice | bytes 25165824 | tf_op jit(solution)/shard_map/reshape | solution.py:53
  113.2 12.6 %copy.60 = f32[12,512,512]{1,2,0:T(8,128)} copy(f32[12,512,512]{2,1,0:T(8,128)} %slice) | data formatting | bytes 25165824 | tf_op jit(solution)/shard_map/reshape | solution.py:53
  126.3 2.1 convolution_convert_fusion.5
  128.8 2.4 convolution_convert_fusion.4
  131.4 49.9 %all-gather.9.cloned.1.call-done = bf16[768,768]{1,0:T(8,128)(2,1)} async-done(((bf16[24,768]{1,0:T(8,128)(2,1)}), bf16[768,768]{1,0:T(8,128)(2,1)}) %all-gather.9.cloned.1.call-update) | async-done | bytes 1179664 | tf_op jit(solution)/shard_map/all_gather | solution.py:187
  181.4 3.0 convolution_convert_fusion.3
  185.8 6.3 fusion.121
  192.0 1.8 fusion.2
  193.9 2.7 copy-done
  196.6 3.2 fusion.62
  199.8 37.9 %all-gather.11.cloned.1.call-done = bf16[768,768]{1,0:T(8,128)(2,1)} async-done(((bf16[24,768]{1,0:T(8,128)(2,1)}), bf16[768,768]{1,0:T(8,128)(2,1)}) %all-gather.11.cloned.1.call-update) | async-done | bytes 1179664 | tf_op jit(solution)/shard_map/all_gather | solution.py:189
  237.7 2.4 multiply_reduce_fusion.3
  241.5 1.6 convolution_convert_fusion.1
  243.1 2.1 reshape.332
  245.3 3.6 all-to-all-start
  249.0 54.9 %all_gather.31 = bf16[768,32]{1,0:T(8,128)(2,1)S(1)} all-gather(bf16[24,32]{1,0:T(8,128)(2,1)S(1)} %convert_element_type.337), channel_id=1, replica_groups=mesh['seq'=32] {'seq'}, dimensions={0}, use_global_device_ids=true | all-gather | bytes 50688 | tf_op jit(solution)/shard_map/all_gather | solution.py:190
  305.4 2.9 convolution_convert_fusion
  308.3 2.1 reshape.337
  310.4 3.4 all-to-all-start.2
  313.8 6.1 fusion.25
  320.0 11.2 %fusion.54 = bf16[32,20,768]{2,0,1:T(8,128)(2,1)S(1)} fusion(f32[1,3072,768]{2,1,0:T(8,128)} %param.27, f32[32,20,3072]{2,0,1:T(8,128)S(1)} %fusion.25), kind=kOutput, calls=%fused_computation.80 | convolution fusion | flops 3040444416 | bytes 18284544 | tf_op jit(solution)/shard_map/secf,efd->secd/dot_general | solution.py:256
  332.7 10.1 %all-to-all-done.2 = bf16[32,20,768]{2,1,0:T(8,128)(2,1)} async-done(((bf16[32,20,768]{2,1,0:T(8,128)(2,1)}), bf16[32,20,768]{2,1,0:T(8,128)(2,1)}, u32[]{:S(2)}, u32[]{:S(2)}) %all-to-all-start.2) | async-done | bytes 983072 | tf_op jit(solution)/shard_map/all_to_all | solution.py:265
  342.9 3.6 all-to-all-start.1
  346.5 10.7 %fusion.28 = bf16[32,20,3072]{2,0,1:T(8,128)(2,1)S(1)} fusion(f32[32,20,3072]{2,0,1:T(8,128)} %copy-done.24, f32[1,3072,768]{2,1,0:T(8,128)} %param.27, bf16[32,20,768]{2,1,0:T(8,128)(2,1)} %all-to-all-done.2), kind=kOutput, calls=%fused_computation.41 | convolution fusion | flops 3057647616 | bytes 22216704 | tf_op jit(solution)/shard_map/secd,efd->secf/dot_general | solution.py:268
  357.3 8.4 fusion.51
  365.7 1.6 copy.65
  367.3 8.3 all-to-all-done.1
  375.6 3.8 all-to-all-start.3
  379.9 2.1 reshape.336
  382.0 3.5 fusion.50
  388.3 20.2 %all-to-all-done.3 = bf16[32,20,768]{2,1,0:T(8,128)(2,1)} async-done(((bf16[32,20,768]{2,1,0:T(8,128)(2,1)}), bf16[32,20,768]{2,1,0:T(8,128)(2,1)}, u32[]{:S(2)}, u32[]{:S(2)}) %all-to-all-start.3) | async-done | bytes 983072 | tf_op jit(solution)/shard_map/all_to_all | solution.py:281
  408.4 2.1 reshape.339
  410.6 3.0 multiply_reduce_fusion.1
  413.6 2.9 convert_add_fusion
  416.6 1.7 convolution_convert_fusion.2
  418.3 2.3 copy.66
  420.6 12.1 %multiply_reduce_fusion = (f32[12,512]{1,0:T(8,128)S(1)}, f32[12,512,512]{1,2,0:T(8,128)}) fusion(f32[12,512,512]{1,2,0:T(8,128)} %copy-done, f32[12,512]{1,0:T(8,128)S(1)} %log_add_fusion, bf16[512,12,64]{0,2,1:T(8,128)(2,1)} %bitcast.147, bf16[512,12,64]{0,2,1:T(8,128)(2,1)} %bitcast.156), kind=kOutput, calls=%fused_computation.4 | convolution fusion | flops 412084224 | bytes 26787840 | tf_op jit(solution)/shard_map/while/body/eval_jaxpr/qhd,khd->hqk/dot_general | solution.py:110
  432.8 6.8 multiply_convert_fusion
  439.6 2.6 copy-done.1
  442.2 2.0 multiply_convert_fusion.2
  444.3 3.5 fusion.116
  448.9 4.8 multiply_convert_fusion.1
  454.7 2.4 fusion.114
  458.2 6.7 fusion.59
  465.8 2.5 fusion.112
  468.4 10.6 %convolution_bitcast_fusion = f32[1,768,3072]{2,1,0:T(8,128)} fusion(bf16[32,20,768]{2,1,0:T(8,128)(2,1)} %all-to-all-done, bf16[32,20,3072]{2,0,1:T(8,128)(2,1)} %copy-done.25), kind=kOutput, calls=%fused_computation.31 | convolution fusion | flops 3019898880 | bytes 14352384 | tf_op jit(solution)/shard_map/secd,secf->edf/dot_general | solution.py:275
  479.0 2.2 fusion.96
  481.2 12.4 %convolution_bitcast_fusion.1 = f32[1,3072,768]{2,1,0:T(8,128)} fusion(f32[32,20,3072]{2,0,1:T(8,128)} %copy-done.24, bf16[32,20,768]{2,1,0:T(8,128)(2,1)} %all-to-all-done.2), kind=kOutput, calls=%fused_computation.32 | convolution fusion | flops 3037593600 | bytes 18284544 | tf_op jit(solution)/shard_map/secf,secd->efd/dot_general | solution.py:272
  493.6 14.7 %copy.71 = bf16[12,512,512]{2,0,1:T(8,128)(2,1)} copy(bf16[12,512,512]{1,2,0:T(8,128)(2,1)} %copy-done.1) | data formatting | bytes 12582912 | tf_op jit(solution)/shard_map/while/body/eval_jaxpr/convert_element_type | solution.py:120
  508.3 18.4 %fusion.65 = f32[32,12]{1,0:T(8,128)S(1)} fusion(bf16[12,512,512]{2,0,1:T(8,128)(2,1)} %copy.71, pred[32,512,512]{2,1,0:T(32,128)(4,1)} %iota_compare_fusion), kind=kOutput, calls=%fused_computation.91 | convolution fusion | flops 201326592 | bytes 14681600 | tf_op jit(solution)/shard_map/while/body/eval_jaxpr/dot_general | solution.py:129
  526.8 2.2 fusion.124
  530.6 2.4 fusion.47
  533.0 38.3 %all-reduce.7 = (f32[768]{0:T(1024)S(1)}, f32[768]{0:T(1024)S(1)}, f32[384]{0:T(512)S(1)}) all-reduce(f32[768]{0:T(1024)S(1)} %get-tuple-element.64, f32[768]{0:T(1024)S(1)} %get-tuple-element.62, f32[384]{0:T(512)S(1)} %reshape.341), channel_id=2, replica_groups=mesh['seq'=32] {'seq'}, use_global_device_ids=true, to_apply=%region_13.14.clone | all-reduce | flops 1920 | bytes 15360
  573.0 2.7 fusion.46
  575.8 67.2 %reduce-scatter.8.cloned.1.call-done = f32[24,768]{1,0:T(8,128)} async-done(((f32[768,768]{1,0:T(8,128)}), f32[24,768]{1,0:T(8,128)}) %reduce-scatter.8.cloned.1.call-update) | async-done | bytes 73744 | tf_op jit(solution)/shard_map/reduce_scatter | solution.py:336
  643.0 104.0 %reduce-scatter.10.cloned.1.call-done = f32[24,768]{1,0:T(8,128)} async-done(((f32[768,768]{1,0:T(8,128)}), f32[24,768]{1,0:T(8,128)}) %reduce-scatter.10.cloned.1.call-update) | async-done | bytes 73744 | tf_op jit(solution)/shard_map/reduce_scatter | solution.py:337
  747.0 104.7 %reduce-scatter.12.cloned.1.call-done = f32[24,768]{1,0:T(8,128)} async-done(((f32[768,768]{1,0:T(8,128)}), f32[24,768]{1,0:T(8,128)}) %reduce-scatter.12.cloned.1.call-update) | async-done | bytes 73744 | tf_op jit(solution)/shard_map/reduce_scatter | solution.py:338
  851.7 104.0 %reduce-scatter.14.cloned.1.call-done = f32[24,768]{1,0:T(8,128)} async-done(((f32[768,768]{1,0:T(8,128)}), f32[24,768]{1,0:T(8,128)}) %reduce-scatter.14.cloned.1.call-update) | async-done | bytes 73744 | tf_op jit(solution)/shard_map/reduce_scatter | solution.py:339
  (120 shorter events, 26.1 us)
Async XLA Ops:
  7.2 51.7 %copy-start.2 = (bf16[512,768]{1,0:T(8,128)(2,1)S(1)}, bf16[512,768]{1,0:T(8,128)(2,1)}, u32[]{:S(2)}) copy-start(bf16[512,768]{1,0:T(8,128)(2,1)} %param.14) | copy-start | bytes 2359300
  7.2 119.1 %all-gather.5.cloned.1.call-start = ((), (), s32[]{:S(2)}) async-start(), calls=%async_computation.9 | async-start | bytes 1216512 | tf_op jit(solution)/shard_map/all_gather | solution.py:188
  8.8 119.9 %all-gather.7.cloned.1.call-start = ((), (), s32[]{:S(2)}) async-start(), calls=%async_computation.10 | async-start | bytes 1216512 | tf_op jit(solution)/shard_map/all_gather | solution.py:186
  10.4 170.9 %all-gather.9.cloned.1.call-start = ((), (), s32[]{:S(2)}) async-start(), calls=%async_computation.11 | async-start | bytes 1216512 | tf_op jit(solution)/shard_map/all_gather | solution.py:187
  12.0 225.7 %all-gather.11.cloned.1.call-start = ((), (), s32[]{:S(2)}) async-start(), calls=%async_computation.12 | async-start | bytes 1216512 | tf_op jit(solution)/shard_map/all_gather | solution.py:189
  113.1 12.6 %copy-start.21 = (s32[1,512]{1,0:T(1,128)S(1)}, s32[1,512]{1,0:T(1,128)}, u32[]{:S(2)}) copy-start(s32[1,512]{1,0:T(1,128)} %param.15) | copy-start | bytes 6148
  113.2 12.9 %copy-start.19 = (s32[512,1]{0,1:T(1,128)S(1)}, s32[512,1]{0,1:T(1,128)}, u32[]{:S(2)}) copy-start(s32[512,1]{0,1:T(1,128)} %param.16) | copy-start | bytes 6148
  128.7 65.1 %copy-start.12 = (bf16[512,768]{0,1:T(8,128)(2,1)}, bf16[512,768]{0,1:T(8,128)(2,1)S(1)}, u32[]{:S(2)}) copy-start(bf16[512,768]{0,1:T(8,128)(2,1)S(1)} %copy.57) | copy-start | bytes 2359300
  131.4 54.3 %copy-start.5 = (bf16[512,768]{0,1:T(8,128)(2,1)}, bf16[512,768]{0,1:T(8,128)(2,1)S(1)}, u32[]{:S(2)}) copy-start(bf16[512,768]{0,1:T(8,128)(2,1)S(1)} %copy.58) | copy-start | bytes 2359300
  192.0 4.5 copy-start
  240.1 170.5 %copy-start.3 = (f32[512,768]{1,0:T(8,128)}, f32[512,768]{1,0:T(8,128)S(1)}, u32[]{:S(2)}) copy-start(f32[512,768]{1,0:T(8,128)S(1)} %get-tuple-element.90) | copy-start | bytes 4718596
  240.3 1.1 copy-start.7
  243.1 5.8 copy-start.20
  245.3 65.2 %all-to-all-start = ((bf16[32,20,768]{2,1,0:T(8,128)(2,1)}), bf16[32,20,768]{2,1,0:T(8,128)(2,1)}, u32[]{:S(2)}, u32[]{:S(2)}) async-start(bf16[32,20,768]{2,1,0:T(8,128)(2,1)} %reshape.332), calls=%async_computation | async-start | bytes 2359296 | tf_op jit(solution)/shard_map/all_to_all | solution.py:249
  310.4 32.4 %all-to-all-start.2 = ((bf16[32,20,768]{2,1,0:T(8,128)(2,1)}), bf16[32,20,768]{2,1,0:T(8,128)(2,1)}, u32[]{:S(2)}, u32[]{:S(2)}) async-start(bf16[32,20,768]{2,1,0:T(8,128)(2,1)} %reshape.337), calls=%async_computation.2 | async-start | bytes 2359296 | tf_op jit(solution)/shard_map/all_to_all | solution.py:265
  320.0 11.2 %copy-start.24 = (f32[32,20,3072]{2,0,1:T(8,128)}, f32[32,20,3072]{2,0,1:T(8,128)S(1)}, u32[]{:S(2)}) copy-start(f32[32,20,3072]{2,0,1:T(8,128)S(1)} %fusion.25) | copy-start | bytes 23592964
  342.9 32.7 %all-to-all-start.1 = ((bf16[32,20,768]{2,1,0:T(8,128)(2,1)}), bf16[32,20,768]{2,1,0:T(8,128)(2,1)}, u32[]{:S(2)}, u32[]{:S(2)}) async-start(bf16[32,20,768]{2,1,0:T(8,128)(2,1)} %copy.63), calls=%async_computation.1 | async-start | bytes 2359296 | tf_op jit(solution)/shard_map/all_to_all | solution.py:259
  357.3 8.4 copy-start.25
  375.6 32.8 %all-to-all-start.3 = ((bf16[32,20,768]{2,1,0:T(8,128)(2,1)}), bf16[32,20,768]{2,1,0:T(8,128)(2,1)}, u32[]{:S(2)}, u32[]{:S(2)}) async-start(bf16[32,20,768]{2,1,0:T(8,128)(2,1)} %copy.65), calls=%async_computation.3 | async-start | bytes 2359296 | tf_op jit(solution)/shard_map/all_to_all | solution.py:281
  379.4 196.4 %reduce-scatter.16.cloned.1.call-start = ((), (), s32[]{:S(2)}) async-start(), calls=%async_computation.17 | async-start | bytes 405504
  382.0 3.5 copy-start.8
  410.6 3.0 copy-start.15
  410.6 3.0 copy-start.17
  413.6 3.0 copy-start.23
  420.6 12.1 %slice-start = ((s8[12582912]{0:T(1024)(128)(4,1)}), s8[4194304]{0:T(1024)(128)(4,1)S(1)}, s32[]{:S(2)}) async-start(s8[12582912]{0:T(1024)(128)(4,1)} %bitcast.139), calls=%async_computation.18 | async-start | bytes 8388608
  420.6 12.2 %slice-start.1 = ((s8[12582912]{0:T(1024)(128)(4,1)}), s8[4194304]{0:T(1024)(128)(4,1)S(1)}, s32[]{:S(2)}) async-start(s8[12582912]{0:T(1024)(128)(4,1)} %bitcast.139), calls=%async_computation.19 | async-start | bytes 8388608
  420.6 12.2 %slice-start.2 = ((s8[12582912]{0:T(1024)(128)(4,1)}), s8[4194304]{0:T(1024)(128)(4,1)S(1)}, s32[]{:S(2)}) async-start(s8[12582912]{0:T(1024)(128)(4,1)} %bitcast.139), calls=%async_computation.20 | async-start | bytes 8388608
  439.6 2.6 copy-start.1
  444.2 198.8 %reduce-scatter.8.cloned.1.call-start = ((), (), s32[]{:S(2)}) async-start(), calls=%async_computation.13 | async-start | bytes 2433024 | tf_op jit(solution)/shard_map/reduce_scatter | solution.py:336
  447.8 1.1 copy-start.6
  447.8 299.2 %reduce-scatter.10.cloned.1.call-start = ((), (), s32[]{:S(2)}) async-start(), calls=%async_computation.14 | async-start | bytes 2433024 | tf_op jit(solution)/shard_map/reduce_scatter | solution.py:337
  453.7 0.9 copy-start.13
  457.1 1.1 copy-start.4
  457.1 394.6 %reduce-scatter.12.cloned.1.call-start = ((), (), s32[]{:S(2)}) async-start(), calls=%async_computation.15 | async-start | bytes 2433024 | tf_op jit(solution)/shard_map/reduce_scatter | solution.py:338
  464.9 0.9 copy-start.9
  468.3 10.7 %copy-start.18 = (bf16[12,64,512]{2,1,0:T(8,128)(2,1)S(1)}, bf16[12,64,512]{2,1,0:T(8,128)(2,1)}, u32[]{:S(2)}) copy-start(bf16[12,64,512]{2,1,0:T(8,128)(2,1)} %fusion.62) | copy-start | bytes 2359300
  468.3 487.4 %reduce-scatter.14.cloned.1.call-start = ((), (), s32[]{:S(2)}) async-start(), calls=%async_computation.16 | async-start | bytes 2433024 | tf_op jit(solution)/shard_map/reduce_scatter | solution.py:339
  508.3 18.5 %copy-start.11 = (bf16[12,64,512]{2,1,0:T(8,128)(2,1)S(1)}, bf16[12,64,512]{2,1,0:T(8,128)(2,1)}, u32[]{:S(2)}) copy-start(bf16[12,64,512]{2,1,0:T(8,128)(2,1)} %multiply_convert_fusion.2) | copy-start | bytes 2359300
  526.8 2.3 copy-start.14
  526.8 2.3 copy-start.22
  529.1 1.1 copy-start.10
  529.1 1.5 copy-start.16
Sparse Core Ops, SparseCore 0:
  11.5 56.7 all-gather.4
  71.7 53.0 all-gather.6
  128.4 52.9 all-gather.8
  184.7 52.9 all-gather.10
  444.4 93.8 reduce-scatter.15
  544.9 98.0 reduce-scatter.7
  648.9 98.1 reduce-scatter.9
  753.7 97.9 reduce-scatter.11
  857.6 98.1 reduce-scatter.13
where the time goes:
time: 974 us; the launch traced here: 963 us
  waiting for transfers between devices  507 us (52%)
  matrix products  164 us (17%)
  blocking collectives  135 us (14%)
  local copies, waits for them, and re-layouts  95 us (10%)
  other arithmetic  31.9 us (3%)
  starting transfers between devices  15.4 us (2%)
  between operations  14.7 us (2%)
    reduce_scatter x1, waiting for transfers between devices, shards(): lax.psum_scatter(grad_value_w, 'seq', scatter_dimension=0, tiled=True)  105 us
    reduce_scatter x1, waiting for transfers between devices, shards(): lax.psum_scatter(grad_output_w, 'seq', scatter_dimension=0, tiled=True)  104 us
    reduce_scatter x1, waiting for transfers between devices, shards(): lax.psum_scatter(grad_key_w, 'seq', scatter_dimension=0, tiled=True)  104 us
    unnamed x2, blocking collectives  80.4 us
    reduce_scatter x1, waiting for transfers between devices, shards(): lax.psum_scatter(grad_query_w, 'seq', scatter_dimension=0, tiled=True)  67.2 us
    all_gather x1, blocking collectives, shards(): lax.all_gather(w_router.astype(jnp.bfloat16), 'seq', axis=0, tiled=True)  54.9 us
    all_gather x1, waiting for transfers between devices, shards(): lax.all_gather(w_key.astype(jnp.bfloat16), 'seq', axis=0, tiled=True)  49.9 us
    unnamed x69, local copies, waits for them, and re-layouts  40.9 us
  transfers between devices with their start and end apart: 13, of which 9 were waited for; matrix products, arithmetic and copies ran while one was open for 25% of the time, Pallas kernels for 0%

commit v1 on v0

v1 whole, which is shorter than its diff:
```python
import functools

import jax
import jax.numpy as jnp
import numpy as np
from jax import lax
from jax.experimental import pallas as pl
from jax.experimental.pallas import tpu as pltpu
from jax.sharding import PartitionSpec as P

HEADS = 12
HEAD_DIM = 64
BUCKETS = 32
GROUPS = 3
LANES = 128

epsilon = 1e-06
bucket_edges = (1, 2, 3, 4, 5, 6, 7, 8, 12, 16, 23, 32, 46, 64, 91)
gelu_coef = 0.7978845608028654
cubic_coef = 0.044715

f32 = jnp.float32
bf16 = jnp.bfloat16


def bit_groups(count):
    bits = count.bit_length() - 1
    groups, low = [(0, 1)], 1
    while low < bits:
        width = min(2, bits - low)
        groups.append((low, width))
        low += width
    return groups


def relative_order(count):
    order = [0]
    for low, width in bit_groups(count):
        order = [base + (m << low) for base in order for m in range(1 << width)]
    return order


def swap(values, distance, count):
    return lax.ppermute(values, "seq", [(i, i ^ distance) for i in range(count)])


def gather_relative(shard, count):
    held = shard
    for low, width in reversed(bit_groups(count)[1:]):
        held = jnp.concatenate(
            [held] + [swap(held, m << low, count) for m in range(1, 1 << width)], axis=0
        )
    return held, swap(held, 1, count)


def scatter_relative(keep, send, count):
    total = keep + swap(send, 1, count).astype(f32)
    for low, width in bit_groups(count)[1:]:
        part = total.shape[0] >> width
        pieces = [total[m * part : (m + 1) * part] for m in range(1 << width)]
        total = pieces[0]
        for m in range(1, 1 << width):
            total = total + swap(pieces[m].astype(bf16), m << low, count).astype(f32)
    return total


def mm(left, right):
    return jnp.dot(left, right, preferred_element_type=f32)


def mm_nt(left, right):
    return lax.dot_general(left, right, (((1,), (1,)), ((), ())), preferred_element_type=f32)


def mm_tn(left, right):
    return lax.dot_general(left, right, (((0,), (0,)), ((), ())), preferred_element_type=f32)


def split_two(values):
    high = values.astype(bf16)
    return high, (values - high.astype(f32)).astype(bf16)


def kernel_call(body, outs, scratch=(), grid=None, in_specs=None, out_specs=None, flops=0, nbytes=0, vmem=48):
    extra = {}
    if grid is not None:
        extra = dict(grid=grid, in_specs=in_specs, out_specs=out_specs)
    return pl.pallas_call(
        body,
        out_shape=[jax.ShapeDtypeStruct(s, d) for s, d in outs],
        scratch_shapes=list(scratch),
        compiler_params=pltpu.CompilerParams(vmem_limit_bytes=vmem * 1024 * 1024),
        cost_estimate=pl.CostEstimate(flops=flops, bytes_accessed=nbytes, transcendentals=0),
        **extra,
    )


def to_slab(values, stage, out_ref):
    slots, width = values.shape
    blocks = width // LANES
    for c in range(blocks):
        stage[pl.ds(c, slots, stride=blocks), :] = values[:, c * LANES : (c + 1) * LANES]
    out_ref[...] = stage[...].astype(out_ref.dtype)


def from_slab(in_ref, stage, slots, put):
    stage[...] = in_ref[...].astype(f32)
    blocks = in_ref.shape[0] // slots
    for c in range(blocks):
        put(c, stage[pl.ds(c, slots, stride=blocks), :])


def to_column(row, width=LANES):
    return jnp.transpose(jnp.broadcast_to(row, (width, row.shape[1])))


def inverse_rms(values):
    return lax.rsqrt(jnp.mean(values * values, axis=-1, keepdims=True) + epsilon)


def buckets_of(offset):
    magnitude = jnp.abs(offset)
    bucket = jnp.zeros(offset.shape, jnp.int32)
    for edge in bucket_edges:
        bucket = bucket + (magnitude >= edge).astype(jnp.int32)
    return bucket + BUCKETS // 2 * (offset > 0).astype(jnp.int32)


def prepare_kernel(
    rows_local, entries, experts, capacity,
    me_ref, rel_ref, off_ref, x_ref, seg_ref, routes_ref, cot_ref,
    perm_ref, xperm_ref, segcol_ref, hmask_ref, umask_ref, dt_ref, dm_ref, cot_send_ref,
    stage,
):
    tokens, width = x_ref.shape
    slots = dm_ref.shape[0]
    me = me_ref[0]
    device_row = rel_ref[...] ^ me
    off_row = off_ref[...]
    true_row = device_row * rows_local + off_row
    perm = (lax.broadcasted_iota(jnp.int32, (width, width), 0) == true_row).astype(f32).astype(bf16)
    perm_ref[...] = perm
    xperm_ref[...] = mm(x_ref[...], perm).astype(bf16)
    segcol_ref[...] = to_column(seg_ref[...].astype(f32))
    flat = device_row * entries + off_row
    bucket_row = ((flat.astype(f32) + 0.5) * (1.0 / HEADS)).astype(jnp.int32)
    head_row = jnp.where(off_row < entries, flat - bucket_row * HEADS, -1)
    bucket_col = to_column(bucket_row.astype(f32))
    head_col = to_column(head_row.astype(f32))
    lane = lax.broadcasted_iota(jnp.int32, (width, LANES), 1).astype(f32)
    hmask_ref[...] = (head_col == lane).astype(f32).astype(bf16)
    umask_ref[...] = (bucket_col == lane).astype(f32).astype(bf16)
    routes = routes_ref[...]
    labels = lax.broadcasted_iota(jnp.int32, (tokens, experts), 1)
    picked = (routes == labels).astype(f32)
    earlier = (
        lax.broadcasted_iota(jnp.int32, (tokens, tokens), 1)
        <= lax.broadcasted_iota(jnp.int32, (tokens, tokens), 0)
    ).astype(f32).astype(bf16)
    counts = mm(earlier, picked.astype(bf16))
    position = jnp.sum(counts * picked, axis=1, keepdims=True) - 1.0
    slot_col = jnp.where(
        position < capacity, routes.astype(f32) * capacity + position, -1.0
    )
    slot_lane = lax.broadcasted_iota(jnp.int32, (tokens, slots), 1).astype(f32)
    dt_ref[...] = (slot_col == slot_lane).astype(f32).astype(bf16)
    slot_row = jnp.transpose(jnp.broadcast_to(slot_col, (tokens, LANES)))[0:1, :]
    slot_sub = lax.broadcasted_iota(jnp.int32, (slots, tokens), 0).astype(f32)
    dispatch = (slot_sub == slot_row).astype(f32).astype(bf16)
    dm_ref[...] = dispatch
    to_slab(mm(dispatch, cot_ref[...]), stage, cot_send_ref)


def strips_of(vec, heads):
    out = []
    for h in heads:
        spread = jnp.broadcast_to(vec[h : h + 1, :], (LANES, 4 * LANES))
        rolled = pltpu.roll(spread, 3 * LANES + 1, 1, stride=1, stride_axis=0)
        out.append(rolled[:, : 3 * LANES])
    return out


def attend_forward_kernel(group, *refs):
    first = group == 0
    if first:
        (xperm_ref, own_ref, oth_ref, hmask_ref, umask_ref, segrow_ref, segcol_ref,
         qkv_ref, probs_ref, mixed_ref, normed_ref, gain_ref, vec_ref) = refs
    else:
        (normed_ref, vec_ref, own_ref, oth_ref, segrow_ref, segcol_ref,
         qkv_ref, probs_ref, mixed_ref) = refs
    half = own_ref.shape[0]
    tokens = segcol_ref.shape[0]
    per_group = HEADS // GROUPS
    span = per_group * HEAD_DIM
    if first:
        packed = jnp.concatenate(
            [own_ref[:, 3 * span :].astype(f32), oth_ref[:, 3 * span :].astype(f32)], axis=0
        )
        packed_row = jnp.transpose(packed)
        gain = packed_row[0:1, :]
        gain_ref[...] = jnp.broadcast_to(gain, gain_ref.shape)
        table_col = packed[:, 1:2]
        spread = (table_col * hmask_ref[...].astype(f32)).astype(bf16)
        table = mm_tn(spread, umask_ref[...])[:16]
        offset = lax.broadcasted_iota(jnp.int32, (LANES, 4 * LANES), 1) - 255
        onehot = (
            lax.broadcasted_iota(jnp.int32, (LANES, 4 * LANES), 0) == buckets_of(offset)
        ).astype(f32).astype(bf16)
        vec_ref[...] = mm(table.astype(bf16), onehot)
        x = xperm_ref[...].astype(f32)
        normed_ref[...] = (x * inverse_rms(x) * gain).astype(bf16)
    normed = normed_ref[...]
    weights_own = own_ref[:, : 3 * span] if first else own_ref[...]
    weights_oth = oth_ref[:, : 3 * span] if first else oth_ref[...]
    qkv = mm(normed[:, :half], weights_own) + mm(normed[:, half:], weights_oth)
    scale = HEAD_DIM ** (-0.5)
    qkv_ref[:, :span] = (qkv[:, :span].astype(bf16) * scale).astype(bf16)
    qkv_ref[:, span:] = qkv[:, span:].astype(bf16)
    vec = vec_ref[...]
    low_half = lax.broadcasted_iota(jnp.int32, (LANES, LANES), 1) < HEAD_DIM
    blocks = tokens // LANES
    for pair in range(span // LANES):
        cols = slice(pair * LANES, (pair + 1) * LANES)
        keys = qkv_ref[:, span + pair * LANES : span + (pair + 1) * LANES]
        vals = qkv_ref[:, 2 * span + pair * LANES : 2 * span + (pair + 1) * LANES]
        heads = [group * per_group + pair * 2 + k for k in range(2)]
        strips = strips_of(vec, heads)
        for i in range(blocks):
            rows = slice(i * LANES, (i + 1) * LANES)
            query = qkv_ref[rows, cols]
            same = segcol_ref[rows, 0:1] == segrow_ref[...].astype(f32)
            mixed = []
            for k in range(2):
                keep = low_half if k == 0 else jnp.logical_not(low_half)
                masked = jnp.where(keep, query, jnp.zeros_like(query))
                scores = mm_nt(masked, keys)
                h = heads[k]
                left = vec[h : h + 1, 0:1]
                right = vec[h : h + 1, 510:511]
                bias = []
                for j in range(blocks):
                    if j < i - 1:
                        bias.append(jnp.broadcast_to(left, (LANES, LANES)))
                    elif j > i + 1:
                        bias.append(jnp.broadcast_to(right, (LANES, LANES)))
                    else:
                        at = (j - i + 1) * LANES
                        bias.append(strips[k][:, at : at + LANES])
                scores = scores + jnp.concatenate(bias, axis=1)
                scores = jnp.where(same, scores, -1000000000.0)
                top = jnp.max(scores, axis=-1, keepdims=True)
                weights = jnp.exp(scores - top)
                total = jnp.sum(weights, axis=-1, keepdims=True)
                probs = (weights * (1.0 / total)).astype(bf16)
                probs_ref[pair * 2 + k, rows, :] = probs
                mixed.append(mm(probs, vals))
            mixed_ref[rows, cols] = jnp.where(low_half, mixed[0], mixed[1]).astype(bf16)


def restore_kernel(own_ref, oth_ref, perm_ref, wo_ref, router_ref, gain_ref, experts):
    half = own_ref.shape[0]
    width = wo_ref.shape[1]
    perm = perm_ref[...]
    true = mm(perm[:, :half], own_ref[...]) + mm(perm[:, half:], oth_ref[...])
    wo_ref[...] = true[:, :width].astype(bf16)
    router_ref[...] = true[:, width:].astype(bf16)
    block = (experts // LANES) * LANES
    lanes = jnp.transpose(true[:, width + block : width + block + LANES])
    gain_ref[...] = jnp.broadcast_to(lanes[experts - block : experts - block + 1, :], gain_ref.shape)


def after_kernel(x_ref, m0, m1, m2, wo_ref, gain_ref, dm_ref, after_ref, low_ref, send_ref, stage):
    span = m0.shape[1]
    after = x_ref[...].astype(f32)
    for c, m in enumerate((m0, m1, m2)):
        after = after + mm(m[...], wo_ref[c * span : (c + 1) * span, :])
    after_ref[...] = after
    low = (after * inverse_rms(after) * gain_ref[0:1, :]).astype(bf16)
    low_ref[...] = low
    to_slab(mm(dm_ref[...], low), stage, send_ref)


def transpose_kernel(m0, m1, m2, perm_ref, normed_ref, mixed_t_ref, normed_t_ref):
    span = m0.shape[1]
    total = None
    for c, m in enumerate((m0, m1, m2)):
        part = mm(m[...], perm_ref[c * span : (c + 1) * span, :])
        total = part if total is None else total + part
    mixed_t_ref[...] = jnp.transpose(total).astype(bf16)
    normed_t_ref[...] = jnp.transpose(normed_ref[...].astype(f32)).astype(bf16)


def early_expert_kernel(recv_ref, win_ref, wout_ref, cot_ref, win_low_ref, wout_low_ref, g_ref, stage):
    slots = cot_ref.shape[0]

    @pl.when(pl.program_id(0) == 0)
    def _():
        def put(c, values):
            cot_ref[:, c * LANES : (c + 1) * LANES] = values.astype(bf16)

        from_slab(recv_ref, stage, slots, put)

    win_low_ref[...] = win_ref[0].astype(bf16)
    wout = wout_ref[0].astype(bf16)
    wout_low_ref[...] = wout
    g_ref[...] = mm_nt(cot_ref[...], wout)


def expert_kernel(
    experts, steps,
    me_ref, recv_ref, cot_ref, win_ref, wout_ref, g_ref, router_ref,
    back_ref, prod_ref, hidden_ref, act_ref, x_ref, rows_ref, glog_ref,
    stage, acc_prod, acc_back, gate_ref,
):
    slots = cot_ref.shape[0]
    step = pl.program_id(0)
    wide = router_ref.shape[1]

    def router_probs():
        logits = mm(x_ref[...], router_ref[...])
        lane = lax.broadcasted_iota(jnp.int32, (slots, wide), 1)
        logits = jnp.where(lane < experts, logits, -jnp.inf)
        weights = jnp.exp(logits - jnp.max(logits, axis=-1, keepdims=True))
        probs = weights / jnp.sum(weights, axis=-1, keepdims=True)
        own = (lane == me_ref[0]).astype(f32)
        return probs, own, jnp.sum(probs * own, axis=-1, keepdims=True)

    @pl.when(step == 0)
    def _():
        def put(c, values):
            x_ref[:, c * LANES : (c + 1) * LANES] = values.astype(bf16)

        from_slab(recv_ref, stage, slots, put)
        _, _, gate = router_probs()
        gate_ref[...] = jnp.broadcast_to(gate, gate_ref.shape)
        rows_ref[...] = (gate * cot_ref[...].astype(f32)).astype(bf16)
        acc_prod[...] = jnp.zeros_like(acc_prod)
        acc_back[...] = jnp.zeros_like(acc_back)

    win = win_ref[...]
    pre = mm(x_ref[...], win)
    squared = pre * pre
    bent = jnp.tanh(gelu_coef * (pre + cubic_coef * squared * pre))
    rise = 0.5 * (1.0 + bent)
    hidden = (pre * rise).astype(bf16)
    slope = rise + 0.5 * pre * (1.0 - bent * bent) * gelu_coef * (1.0 + 3.0 * cubic_coef * squared)
    act = (gate_ref[:, 0:1] * g_ref[...] * slope).astype(bf16)
    hidden_ref[...] = hidden
    act_ref[...] = act
    acc_prod[...] += mm(hidden, wout_ref[...])
    acc_back[...] += mm_nt(act, win)

    @pl.when(step == steps - 1)
    def _():
        probs, own, gate = router_probs()
        produced = acc_prod[...].astype(bf16).astype(f32)
        grad_gate = jnp.sum(cot_ref[...].astype(f32) * produced, axis=-1, keepdims=True)
        grad_logits = (probs * (own - gate) * grad_gate).astype(bf16)
        glog_ref[...] = grad_logits
        back = acc_back[...].astype(bf16).astype(f32) + mm_nt(grad_logits, router_ref[...])
        to_slab(back, stage, back_ref)
        to_slab(produced, stage, prod_ref)


def expert_weights_kernel(
    x_ref, rows_ref, glog_ref, perm_ref, hidden_ref, act_ref, gin_ref, gout_ref, grouter_ref, xt
):
    @pl.when(pl.program_id(0) == 0)
    def _():
        xt[...] = jnp.transpose(x_ref[...].astype(f32)).astype(bf16)
        moved = mm(x_ref[...], perm_ref[...]).astype(bf16)
        grouter_ref[...] = mm_tn(moved, glog_ref[...])

    gout_ref[0] = mm_tn(hidden_ref[...], rows_ref[...])
    gin_ref[0] = mm(xt[...], act_ref[...])


def output_kernel(experts, recv_ref, dt_ref, after_ref, low_ref, router_ref, routes_ref, out_ref, stage, rows):
    def put(c, values):
        rows[:, c * LANES : (c + 1) * LANES] = values.astype(bf16)

    from_slab(recv_ref, stage, dt_ref.shape[1], put)
    produced = mm(dt_ref[...], rows[...])
    logits = mm(low_ref[...], router_ref[...])
    lane = lax.broadcasted_iota(jnp.int32, logits.shape, 1)
    logits = jnp.where(lane < experts, logits, -jnp.inf)
    weights = jnp.exp(logits - jnp.max(logits, axis=-1, keepdims=True))
    own = (lane == routes_ref[...]).astype(f32)
    gate = jnp.sum(weights * own, axis=-1, keepdims=True) / jnp.sum(weights, axis=-1, keepdims=True)
    out_ref[...] = (after_ref[...] + gate * produced).astype(bf16)


def norm_two_kernel(
    experts,
    recv_ref, dt_ref, after_ref, gain_ref, cot_ref, wo_ref, mixed_t_ref, perm_ref, grouter_ref,
    grad_after_ref, grad_mixed_ref, keep_ref, send_ref,
    stage, rows,
):
    def put(c, values):
        rows[:, c * LANES : (c + 1) * LANES] = values.astype(bf16)

    from_slab(recv_ref, stage, dt_ref.shape[1], put)
    grad = mm(dt_ref[...], rows[...])
    after = after_ref[...]
    inverse = inverse_rms(after)
    unit = after * inverse
    scaled = grad * gain_ref[0:1, :]
    back = inverse * (scaled - unit * jnp.mean(scaled * unit, axis=-1, keepdims=True))
    grad_after = cot_ref[...].astype(f32) + back
    grad_after_ref[...] = grad_after
    low = grad_after.astype(bf16)
    grad_mixed_ref[...] = mm_nt(low, wo_ref[...]).astype(bf16)
    half = keep_ref.shape[0]
    width = low.shape[1]
    keep_ref[:, :width] = mm(mixed_t_ref[:half, :], low)
    send_ref[:, :width] = mm(mixed_t_ref[half:, :], low).astype(bf16)
    gain_row = jnp.sum(grad * unit, axis=0, keepdims=True)
    high, rest = split_two(jnp.broadcast_to(gain_row, (8, width)))
    gain_row = (mm(high, perm_ref[...]) + mm(rest, perm_ref[...]))[0:1, :]
    grouter = grouter_ref[...]
    lane = lax.broadcasted_iota(jnp.int32, grouter.shape, 1)
    packed = jnp.where(
        lane < experts, grouter, jnp.where(lane == experts, to_column(gain_row, grouter.shape[1]), 0.0)
    )
    keep_ref[:, width:] = packed[:half]
    send_ref[:, width:] = packed[half:].astype(bf16)


def unskew(skewed):
    span = 4 * LANES
    total = None
    for g in range(LANES // 8):
        moved = pltpu.roll(skewed[8 * g : 8 * g + 8, :], (LANES - 1 - 8 * g) % span, 1)
        total = moved if total is None else total + moved
    turned = jnp.concatenate([total[7 - s : 8 - s, :] for s in range(8)], axis=0)
    turned = pltpu.roll(turned, span - 7, 1, stride=1, stride_axis=0)
    return jnp.sum(turned, axis=0, keepdims=True)


def attend_backward_kernel(
    qkv_ref, probs_ref, gm_ref, normed_t_ref,
    dqkv_ref, keep_ref, send_ref, dvec_ref,
    ds_ref,
):
    tokens = qkv_ref.shape[0]
    span = gm_ref.shape[1]
    blocks = tokens // LANES
    scale = HEAD_DIM ** (-0.5)
    low_half = lax.broadcasted_iota(jnp.int32, (LANES, LANES), 1) < HEAD_DIM
    lane = lax.broadcasted_iota(jnp.int32, (1, 4 * LANES), 1)
    for pair in range(span // LANES):
        cols = slice(pair * LANES, (pair + 1) * LANES)
        keys = qkv_ref[:, span + pair * LANES : span + (pair + 1) * LANES]
        vals = qkv_ref[:, 2 * span + pair * LANES : 2 * span + (pair + 1) * LANES]
        query_t = jnp.transpose(qkv_ref[:, cols].astype(f32)).astype(bf16)
        grad_t = jnp.transpose(gm_ref[:, cols].astype(f32)).astype(bf16)
        dq = [[None, None] for _ in range(blocks)]
        dk_t, dv_t = [], []
        for k in range(2):
            head = pair * 2 + k
            keep = low_half if k == 0 else jnp.logical_not(low_half)
            strip = [None] * 3
            far_left = far_right = None
            for i in range(blocks):
                rows = slice(i * LANES, (i + 1) * LANES)
                grad = gm_ref[rows, cols]
                grad = jnp.where(keep, grad, jnp.zeros_like(grad))
                dp = mm_nt(grad, vals)
                probs = probs_ref[head, rows, :].astype(f32)
                delta = jnp.sum(probs * dp, axis=-1, keepdims=True)
                ds = (probs * (dp - delta)).astype(bf16)
                ds_ref[k, rows, :] = ds
                dq[i][k] = mm(ds, keys)
                wide = ds.astype(f32)
                for j in range(blocks):
                    piece = wide[:, j * LANES : (j + 1) * LANES]
                    if j < i - 1:
                        far_left = piece if far_left is None else far_left + piece
                    elif j > i + 1:
                        far_right = piece if far_right is None else far_right + piece
                    else:
                        at = j - i + 1
                        strip[at] = piece if strip[at] is None else strip[at] + piece
            part = slice(k * HEAD_DIM, (k + 1) * HEAD_DIM)
            dk_t.append(mm(query_t[part, :], ds_ref[k]))
            dv_t.append(mm(grad_t[part, :], probs_ref[head]))
            skewed = jnp.concatenate(strip + [jnp.zeros((LANES, LANES), f32)], axis=1)
            vec = unskew(skewed)
            left = jnp.sum(jnp.sum(far_left, axis=0, keepdims=True), axis=1, keepdims=True)
            right = jnp.sum(jnp.sum(far_right, axis=0, keepdims=True), axis=1, keepdims=True)
            vec = vec + jnp.where(lane == 0, left, 0.0) + jnp.where(lane == 510, right, 0.0)
            dvec_ref[head : head + 1, :] = vec
        for i in range(blocks):
            rows = slice(i * LANES, (i + 1) * LANES)
            dqkv_ref[rows, cols] = (jnp.where(low_half, dq[i][0], dq[i][1]) * scale).astype(bf16)
        dk = jnp.transpose(jnp.concatenate(dk_t, axis=0))
        dv = jnp.transpose(jnp.concatenate(dv_t, axis=0))
        dqkv_ref[:, span + pair * LANES : span + (pair + 1) * LANES] = dk.astype(bf16)
        dqkv_ref[:, 2 * span + pair * LANES : 2 * span + (pair + 1) * LANES] = dv.astype(bf16)
    half = keep_ref.shape[0]
    grads = dqkv_ref[...]
    send_ref[...] = mm(normed_t_ref[half:, :], grads).astype(bf16)
    keep_ref[...] = mm(normed_t_ref[:half, :], grads)


def last_kernel(
    xperm_ref, gain_ref, perm_ref, after_ref, hmask_ref, umask_ref,
    d0, own0, oth0, v0, d1, own1, oth1, v1, d2, own2, oth2, v2,
    out_ref, keep_ref, send_ref,
):
    groups = ((d0, own0, oth0, v0), (d1, own1, oth1, v1), (d2, own2, oth2, v2))
    wide = d1.shape[1]
    first = second = None
    for d, own, oth, _ in groups:
        grads = d[...]
        one = mm_nt(grads, own[:, :wide])
        two = mm_nt(grads, oth[:, :wide])
        first = one if first is None else first + one
        second = two if second is None else second + two
    grad = jnp.concatenate([first, second], axis=1)
    x = xperm_ref[...].astype(f32)
    inverse = inverse_rms(x)
    unit = x * inverse
    scaled = grad * gain_ref[0:1, :]
    back = inverse * (scaled - unit * jnp.mean(scaled * unit, axis=-1, keepdims=True))
    high, rest = split_two(back)
    perm = perm_ref[...]
    out_ref[...] = (after_ref[...] + (mm_nt(high, perm) + mm_nt(rest, perm))).astype(bf16)
    gain_col = to_column(jnp.sum(grad * unit, axis=0, keepdims=True))
    per_group = HEADS // GROUPS
    vec = jnp.concatenate(
        [g[3][:per_group, :] for g in groups] + [jnp.zeros((4, 4 * LANES), f32)], axis=0
    )
    offset = lax.broadcasted_iota(jnp.int32, (LANES, 4 * LANES), 1) - 255
    onehot = (
        lax.broadcasted_iota(jnp.int32, (LANES, 4 * LANES), 0) == buckets_of(offset)
    ).astype(f32).astype(bf16)

    def exact(values, right, product):
        one, low = split_two(values)
        two, three = split_two(values - one.astype(f32))
        return product(one, right) + (product(two, right) + product(three, right))

    table = exact(vec, onehot, mm_nt)
    heads = hmask_ref[:, :16]
    one, _ = split_two(table)
    two, _ = split_two(table - one.astype(f32))
    three = (table - one.astype(f32) - two.astype(f32)).astype(bf16)
    spread = mm(heads, one) + (mm(heads, two) + mm(heads, three))
    table_col = jnp.sum(spread * umask_ref[...].astype(f32), axis=1, keepdims=True)
    lane = lax.broadcasted_iota(jnp.int32, gain_col.shape, 1)
    packed = jnp.where(lane == 0, gain_col, jnp.where(lane == 1, table_col, 0.0))
    half = keep_ref.shape[0]
    keep_ref[...] = packed[:half]
    send_ref[...] = packed[half:].astype(bf16)


def shards(
    count,
    inputs,
    segment_ids,
    routes,
    cotangent,
    gain_attn,
    gain_ffn,
    bias_table,
    w_query,
    w_key,
    w_value,
    w_output,
    w_router,
    w_in,
    w_out,
):
    tokens, width = inputs.shape
    experts = w_router.shape[1]
    rows_local = w_query.shape[0]
    entries = bias_table.shape[0]
    hidden_units = w_in.shape[2]
    capacity = max(2, 5 * tokens // (4 * experts))
    slots = experts * capacity
    blocks = width // LANES
    span = width // GROUPS
    half = width // 2
    wide = -(-(experts + 1) // LANES) * LANES
    me = lax.axis_index("seq").astype(jnp.int32).reshape(1)
    smem = pl.BlockSpec(memory_space=pltpu.SMEM)
    vmem = pl.BlockSpec(memory_space=pltpu.VMEM)

    low = [w.astype(bf16) for w in (w_query, w_key, w_value)]
    small = jnp.concatenate(
        [
            gain_attn.astype(bf16)[:, None],
            jnp.pad(bias_table.astype(bf16), (0, rows_local - entries))[:, None],
            jnp.zeros((rows_local, LANES - 2), bf16),
        ],
        axis=1,
    )
    pieces = []
    for c in range(GROUPS):
        own = [w[:, c * span : (c + 1) * span] for w in low]
        pieces.append(jnp.concatenate(own + ([small] if c == 0 else []), axis=1))
    tail = jnp.concatenate(
        [
            w_output.astype(bf16),
            w_router.astype(bf16),
            gain_ffn.astype(bf16)[:, None],
            jnp.zeros((rows_local, wide - experts - 1), bf16),
        ],
        axis=1,
    )
    halves = [gather_relative(p, count) for p in pieces]
    own_tail, oth_tail = gather_relative(tail, count)

    order = np.asarray(relative_order(count), np.int32)
    rel_row = jnp.asarray(np.repeat(order, rows_local)[None, :])
    off_row = jnp.asarray(np.tile(np.arange(rows_local, dtype=np.int32), count)[None, :])
    slab = (slots * blocks, LANES)
    slab_stage = pltpu.VMEM(slab, f32)
    perm, xperm, segcol, hmask, umask, dt, dm, cot_send = pl.pallas_call(
        functools.partial(prepare_kernel, rows_local, entries, experts, capacity),
        out_shape=[
            jax.ShapeDtypeStruct(s, d)
            for s, d in (
                ((width, width), bf16),
                ((tokens, width), bf16),
                ((tokens, LANES), f32),
                ((width, LANES), bf16),
                ((width, LANES), bf16),
                ((tokens, slots), bf16),
                ((slots, tokens), bf16),
                (slab, bf16),
            )
        ],
        in_specs=[smem] + [vmem] * 6,
        scratch_shapes=[slab_stage],
        compiler_params=pltpu.CompilerParams(vmem_limit_bytes=48 * 1024 * 1024),
        cost_estimate=pl.CostEstimate(flops=4 * 10**9, bytes_accessed=10**7, transcendentals=0),
    )(me, rel_row, off_row, inputs, segment_ids, routes, cotangent)

    slab_split = (count, slots * blocks // count, LANES)

    def exchange(rows):
        return lax.all_to_all(
            rows.reshape(slab_split), "seq", split_axis=0, concat_axis=0, tiled=True
        ).reshape(slab)

    cot_recv = exchange(cot_send)

    per_group = HEADS // GROUPS
    group_outs = [
        ((tokens, 3 * span), bf16),
        ((per_group, tokens, tokens), bf16),
        ((tokens, span), bf16),
    ]
    fwd_cost = dict(flops=3 * 10**9, nbytes=8 * 10**6)
    qkv, probs, mixed = [None] * GROUPS, [None] * GROUPS, [None] * GROUPS
    qkv[0], probs[0], mixed[0], normed, gain_one, vec = kernel_call(
        functools.partial(attend_forward_kernel, 0),
        group_outs + [((tokens, width), bf16), ((8, width), f32), ((16, 4 * LANES), f32)],
        **fwd_cost,
    )(xperm, halves[0][0], halves[0][1], hmask, umask, segment_ids, segcol)
    for c in range(1, GROUPS):
        qkv[c], probs[c], mixed[c] = kernel_call(
            functools.partial(attend_forward_kernel, c), group_outs, **fwd_cost
        )(normed, vec, halves[c][0], halves[c][1], segment_ids, segcol)

    output_w, router_w, gain_two = kernel_call(
        functools.partial(restore_kernel, experts=experts),
        [((width, width), bf16), ((width, wide), bf16), ((8, width), f32)],
        flops=10**9,
        nbytes=4 * 10**6,
    )(own_tail, oth_tail, perm)
    after, low_two, row_send = kernel_call(
        after_kernel,
        [((tokens, width), f32), ((tokens, width), bf16), (slab, bf16)],
        scratch=[slab_stage],
        flops=2 * 10**9,
        nbytes=6 * 10**6,
    )(inputs, *mixed, output_w, gain_two, dm)
    row_recv = exchange(row_send)

    step_units = hidden_units // 6
    steps = hidden_units // step_units

    def whole(shape):
        return pl.BlockSpec(shape, lambda i: (0,) * len(shape))

    weight_in = pl.BlockSpec((1, width, step_units), lambda i: (0, 0, i))
    weight_out = pl.BlockSpec((1, step_units, width), lambda i: (0, i, 0))
    low_in = pl.BlockSpec((width, step_units), lambda i: (0, i))
    low_out = pl.BlockSpec((step_units, width), lambda i: (i, 0))
    slot_units = pl.BlockSpec((slots, step_units), lambda i: (0, i))
    cot_rows, win_low, wout_low, grad_hidden = kernel_call(
        early_expert_kernel,
        [
            ((slots, width), bf16),
            ((width, hidden_units), bf16),
            ((hidden_units, width), bf16),
            ((slots, hidden_units), f32),
        ],
        scratch=[slab_stage],
        grid=(steps,),
        in_specs=[whole(slab), weight_in, weight_out],
        out_specs=[whole((slots, width)), low_in, low_out, slot_units],
        flops=3 * 10**9,
        nbytes=36 * 10**6,
    )(cot_recv, w_in, w_out)
    mixed_t, normed_t = kernel_call(
        transpose_kernel,
        [((width, tokens), bf16), ((width, tokens), bf16)],
        flops=10**9,
        nbytes=4 * 10**6,
    )(*mixed, perm, normed)
    back_send, prod_send, hidden, act, x_rows, grad_rows, grad_logits = kernel_call(
        functools.partial(expert_kernel, experts, steps),
        [
            (slab, bf16),
            (slab, bf16),
            ((slots, hidden_units), bf16),
            ((slots, hidden_units), bf16),
            ((slots, width), bf16),
            ((slots, width), bf16),
            ((slots, wide), bf16),
        ],
        scratch=[
            slab_stage,
            pltpu.VMEM((slots, width), f32),
            pltpu.VMEM((slots, width), f32),
            pltpu.VMEM((slots, LANES), f32),
        ],
        grid=(steps,),
        in_specs=[
            smem,
            whole(slab),
            whole((slots, width)),
            low_in,
            low_out,
            slot_units,
            whole((width, wide)),
        ],
        out_specs=[
            whole(slab),
            whole(slab),
            slot_units,
            slot_units,
            whole((slots, width)),
            whole((slots, width)),
            whole((slots, wide)),
        ],
        flops=10 * 10**9,
        nbytes=30 * 10**6,
    )(me, row_recv, cot_rows, win_low, wout_low, grad_hidden, router_w)
    back_recv = exchange(back_send)
    prod_send, back_recv_first = lax.optimization_barrier((prod_send, back_recv))
    prod_recv = exchange(prod_send)
    grad_inner, grad_outer, grad_router = kernel_call(
        expert_weights_kernel,
        [
            ((1, width, hidden_units), f32),
            ((1, hidden_units, width), f32),
            ((width, wide), f32),
        ],
        scratch=[pltpu.VMEM((width, slots), bf16)],
        grid=(steps,),
        in_specs=[
            whole((slots, width)),
            whole((slots, width)),
            whole((slots, wide)),
            whole((width, width)),
            slot_units,
            slot_units,
        ],
        out_specs=[weight_in, weight_out, whole((width, wide))],
        flops=7 * 10**9,
        nbytes=30 * 10**6,
    )(x_rows, grad_rows, grad_logits, perm, hidden, act)

    row_scratch = pltpu.VMEM((slots, width), bf16)
    grad_after, grad_mixed, keep_o, send_o = kernel_call(
        functools.partial(norm_two_kernel, experts),
        [
            ((tokens, width), f32),
            ((tokens, width), bf16),
            ((half, width + wide), f32),
            ((half, width + wide), bf16),
        ],
        scratch=[slab_stage, row_scratch],
        flops=2 * 10**9,
        nbytes=10 * 10**6,
    )(back_recv_first, dt, after, gain_two, cotangent, output_w, mixed_t, perm, grad_router)
    sum_o = scatter_relative(keep_o, send_o, count)

    output = kernel_call(
        functools.partial(output_kernel, experts),
        [((tokens, width), bf16)],
        scratch=[slab_stage, row_scratch],
        flops=10**9,
        nbytes=5 * 10**6,
    )(prod_recv, dt, after, low_two, router_w, routes)[0]

    grads, sums = [], []
    for c in range(GROUPS):
        dqkv, keep, send, dvec = kernel_call(
            attend_backward_kernel,
            [
                ((tokens, 3 * span), bf16),
                ((half, 3 * span), f32),
                ((half, 3 * span), bf16),
                ((8, 4 * LANES), f32),
            ],
            scratch=[pltpu.VMEM((2, tokens, tokens), bf16)],
            flops=4 * 10**9,
            nbytes=8 * 10**6,
        )(qkv[c], probs[c], grad_mixed[:, c * span : (c + 1) * span], normed_t)
        sums.append(scatter_relative(keep, send, count))
        grads += [dqkv, halves[c][0], halves[c][1], dvec]
    grad_inputs, keep, send = kernel_call(
        last_kernel,
        [((tokens, width), bf16), ((half, LANES), f32), ((half, LANES), bf16)],
        flops=4 * 10**9,
        nbytes=10 * 10**6,
    )(xperm, gain_one, perm, grad_after, hmask, umask, *grads)
    sum_small = scatter_relative(keep, send, count)

    def weight(k):
        return jnp.concatenate([s[:, k * span : (k + 1) * span] for s in sums], axis=1)

    return (
        output,
        grad_inputs,
        sum_small[:, 0],
        sum_o[:, width + experts],
        sum_small[:entries, 1],
        weight(0),
        weight(1),
        weight(2),
        sum_o[:, :width],
        sum_o[:, width : width + experts],
        grad_inner,
        grad_outer,
    )


def solution(mesh):
    row, flat, cube = P("seq", None), P("seq"), P("seq", None, None)
    in_specs = (row,) * 4 + (flat,) * 3 + (row,) * 5 + (cube,) * 2
    out_specs = (row,) * 2 + (flat,) * 3 + (row,) * 5 + (cube,) * 2
    return jax.shard_map(
        functools.partial(shards, mesh.shape["seq"]),
        mesh=mesh,
        in_specs=in_specs,
        out_specs=out_specs,
        check_vma=False,
    )
```

time: 974 us -> 359 us (0.37)
  waiting for transfers between devices: 507 us -> 80.3 us
  matrix products: 164 us -> 0 us
  blocking collectives: 135 us -> 0 us
  Pallas kernels: 0 us -> 119 us
  starting transfers between devices: 15.4 us -> 100 us
  local copies, waits for them, and re-layouts: 95 us -> 44.1 us
  other arithmetic: 31.9 us -> 9.23 us
  between operations: 14.7 us -> 1.88 us
    reduce_scatter x4 -> x0, waiting for transfers between devices: 380 us -> none  [the longest x1 105 us: shards(): lax.psum_scatter(grad_value_w, 'seq', scatter_dimension=0, tiled=True)]
    dot_general x34 -> x0, matrix products: 164 us -> none  [the longest x1 18.4 us: attend_backward(): lax.dot_general(onehot, grad_scores.reshape(HEADS, length * length), (((1...]
    pallas_call x0 -> x16, Pallas kernels: none -> 119 us  [the longest x3 23.2 us: shards(): kernel_call(attend_backward_kernel, [((tokens, 3 * span), bf16), ((half,...]
    all_gather x4 -> x0, waiting for transfers between devices: 87.8 us -> none  [the longest x1 49.9 us: shards(): lax.all_gather(w_key.astype(jnp.bfloat16), 'seq', axis=0, tiled=True)]
    ppermute x0 -> x63, starting transfers between devices: none -> 83.6 us  [swap(): lax.ppermute(values, 'seq', [(i, i ^ distance) for i in range(count)])]
    unnamed x2 -> x0, blocking collectives: 80.4 us -> none
    ppermute x0 -> x63, waiting for transfers between devices: none -> 65.7 us  [swap(): lax.ppermute(values, 'seq', [(i, i ^ distance) for i in range(count)])]
    all_gather x1 -> x0, blocking collectives: 54.9 us -> none  [shards(): lax.all_gather(w_router.astype(jnp.bfloat16), 'seq', axis=0, tiled=True)]
  transfers between devices with their start and end apart: 13 -> 67, of which waited for: 9 -> 28; matrix products, arithmetic and copies ran while one was open for 25% -> 3% of each run, Pallas kernels for 0% -> 17%
where the time goes in v1:
time: 359 us; the launch traced here: 355 us
  Pallas kernels  119 us (33%)
  starting transfers between devices  100 us (28%)
  waiting for transfers between devices  80.3 us (22%)
  local copies, waits for them, and re-layouts  44.1 us (12%)
  other arithmetic  9.23 us (3%)
    ppermute x63, starting transfers between devices, swap(): lax.ppermute(values, 'seq', [(i, i ^ distance) for i in range(count)])  83.6 us
    ppermute x63, waiting for transfers between devices, swap(): lax.ppermute(values, 'seq', [(i, i ^ distance) for i in range(count)])  65.7 us
    unnamed x186, local copies, waits for them, and re-layouts  40.1 us
    pallas_call x3, Pallas kernels, shards(): kernel_call(attend_backward_kernel, [((tokens, 3 * span), bf16), ((half,...  23.2 us
    pallas_call x1, Pallas kernels, shards(): kernel_call(functools.partial(expert_kernel, experts, steps), [(slab, bf1...  20.1 us
    all_to_all x4, starting transfers between devices, exchange(): lax.all_to_all(rows.reshape(slab_split), 'seq', split_axis=0, concat_axis...  16.6 us
    all_to_all x4, waiting for transfers between devices, exchange(): lax.all_to_all(rows.reshape(slab_split), 'seq', split_axis=0, concat_axis...  14.6 us
    pallas_call x1, Pallas kernels, shards(): kernel_call(expert_weights_kernel, [((1, width, hidden_units), f32), ((1,...  14.3 us
  transfers between devices with their start and end apart: 67, of which 28 were waited for; matrix products, arithmetic and copies ran while one was open for 3% of the time, Pallas kernels for 17%

profile of v1, /device:TPU:0, one launch (start us, length us, event | category | flops | bytes accessed | tf_op | source)
XLA Modules:
  0.0 354.7 jit_solution(12553828572803845687)
XLA Ops:
  5.0 5.1 %collective-permute-start.2 = (bf16[24,896]{1,0:T(8,128)(2,1)S(1)}, bf16[24,896]{1,0:T(8,128)(2,1)S(1)}, u32[]{:S(2)}, u32[]{:S(2)}) collective-permute-start(bf16[24,896]{1,0:T(8,128)(2,1)S(1)} %concatenate.49), channel_id=1, source_target_pairs={{0,24},{1,25},{2,26},{3,27},{4,28},{5,29},{6,30},{7,31},{8,16},{9,... | collective-permute-start | bytes 129032 | tf_op jit(solution)/shard_map/ppermute | solution.py:44
  11.3 2.3 collective-permute-start.15
  13.6 2.0 collective-permute-start.14
  20.8 2.9 shard_map.247
  26.7 3.0 all-to-all-start.1
  30.0 3.7 %collective-permute-start.16 = (bf16[24,768]{1,0:T(8,128)(2,1)S(1)}, bf16[24,768]{1,0:T(8,128)(2,1)S(1)}, u32[]{:S(2)}, u32[]{:S(2)}) collective-permute-start(bf16[24,768]{1,0:T(8,128)(2,1)S(1)} %get-tuple-element.199), channel_id=1, source_target_pairs={{0,24},{1,25},{2,26},{3,27},{4,28},{5,29},{6,30},{7,31},{8,16},{9,... | collective-permute-start | bytes 110600 | tf_op jit(solution)/shard_map/ppermute | solution.py:44
  34.9 16.3 %collective-permute-done.16 = bf16[24,768]{1,0:T(8,128)(2,1)S(1)} collective-permute-done((bf16[24,768]{1,0:T(8,128)(2,1)S(1)}, bf16[24,768]{1,0:T(8,128)(2,1)S(1)}, u32[]{:S(2)}, u32[]{:S(2)}) %collective-permute-start.16) | collective-permute-done | bytes 36896 | tf_op jit(solution)/shard_map/ppermute | solution.py:44
  51.3 6.5 %collective-permute-start.7 = (bf16[24,768]{1,0:T(8,128)(2,1)S(1)}, bf16[24,768]{1,0:T(8,128)(2,1)S(1)}, u32[]{:S(2)}, u32[]{:S(2)}) collective-permute-start(bf16[24,768]{1,0:T(8,128)(2,1)S(1)} %get-tuple-element.210), channel_id=1, source_target_pairs={{0,8},{1,9},{2,10},{3,11},{4,12},{5,13},{6,14},{7,15},{8,0},{9,1},... | collective-permute-start | bytes 110600 | tf_op jit(solution)/shard_map/ppermute | solution.py:44
  60.8 2.4 collective-permute-start.22
  63.2 2.7 collective-permute-done.9
  65.9 1.6 collective-permute-start.23
  67.5 1.8 collective-permute-start.19
  73.7 4.6 %collective-permute-done.3 = bf16[96,896]{1,0:T(8,128)(2,1)S(1)} collective-permute-done((bf16[96,896]{1,0:T(8,128)(2,1)S(1)}, bf16[96,896]{1,0:T(8,128)(2,1)S(1)}, u32[]{:S(2)}, u32[]{:S(2)}) %collective-permute-start.3) | collective-permute-done | bytes 172064 | tf_op jit(solution)/shard_map/ppermute | solution.py:44
  78.3 1.6 collective-permute-start.5
  81.1 3.6 %collective-permute-done.5 = bf16[96,896]{1,0:T(8,128)(2,1)S(1)} collective-permute-done((bf16[96,896]{1,0:T(8,128)(2,1)S(1)}, bf16[96,896]{1,0:T(8,128)(2,1)S(1)}, u32[]{:S(2)}, u32[]{:S(2)}) %collective-permute-start.5) | collective-permute-done | bytes 172064 | tf_op jit(solution)/shard_map/ppermute | solution.py:44
  86.0 1.5 collective-permute-done.24
  87.5 2.1 collective-permute-start.26
  90.1 1.7 collective-permute-start.12
  91.8 2.7 collective-permute-done.26
  97.7 3.2 collective-permute-done.10
  102.1 1.7 shard_map.251
  104.0 8.4 %shard_map.248 = (bf16[512,768]{1,0:T(8,128)(2,1)S(1)}, bf16[4,512,512]{2,1,0:T(8,128)(2,1)}, bf16[512,256]{1,0:T(8,128)(2,1)S(1)}, bf16[512,768]{1,0:T(8,128)(2...) custom-call(bf16[512,768]{1,0:T(8,128)(2,1)S(1)} %copy-done.53, ...), custom_call_target="tpu_custom_call" | custom-call | flops 3000000000 | bytes 8000000 | tf_op jit(solution)/shard_map/pallas_call | solution.py:658
  113.3 7.2 %shard_map.250 = (bf16[512,768]{1,0:T(8,128)(2,1)S(1)}, bf16[4,512,512]{2,1,0:T(8,128)(2,1)S(1)}, bf16[512,256]{1,0:T(8,128)(2,1)S(1)}) custom-call(bf16[512,768]{1,0:T(8,128)(2,1)S(1)} %get-tuple-element.80.refs_0_.normed_ref, f32[16,512]{1,0:T(8,128)S(1)} %get-tuple-element.81.refs_1_, ...), custom_call_target="tpu_custom_call" | custom-call | flops 3000000000 | bytes 8000000 | tf_op jit(solution)/shard_map/pallas_call | solution.py:664
  122.7 6.9 %shard_map.249 = (bf16[512,768]{1,0:T(8,128)(2,1)S(1)}, bf16[4,512,512]{2,1,0:T(8,128)(2,1)S(1)}, bf16[512,256]{1,0:T(8,128)(2,1)S(1)}) custom-call(bf16[512,768]{1,0:T(8,128)(2,1)S(1)} %get-tuple-element.80.refs_0_.normed_ref, f32[16,512]{1,0:T(8,128)S(1)} %get-tuple-element.81.refs_1_, ...), custom_call_target="tpu_custom_call" | custom-call | flops 3000000000 | bytes 8000000 | tf_op jit(solution)/shard_map/pallas_call | solution.py:664
  131.9 2.9 shard_map.252
  137.4 7.1 %all-to-all-start = ((bf16[32,120,128]{2,1,0:T(8,128)(2,1)}), bf16[32,120,128]{2,1,0:T(8,128)(2,1)}, u32[]{:S(2)}, u32[]{:S(2)}) async-start(bf16[32,120,128]{2,1,0:T(8,128)(2,1)} %bitcast.20), calls=%async_computation | async-start | bytes 1966080 | tf_op jit(solution)/shard_map/all_to_all | solution.py:644
  144.5 14.0 %shard_map.253 = (bf16[640,768]{1,0:T(8,128)(2,1)S(1)}, bf16[768,3072]{1,0:T(8,128)(2,1)}, bf16[3072,768]{1,0:T(8,128)(2,1)}, f32[640,3072]{1,0:T(8,128)}) custom-call(bf16[3840,128]{1,0:T(8,128)(2,1)S(1)} %bitcast.16, f32[1,768,3072]{2,1,0:T(8,128)} %win_ref.1, f32[1,3072,768]{2,1,0:T(8,128)} %wout_ref.1), custom_call_target="tpu_custom_call" | custom-call | flops 3000000000 | bytes 36000000 | tf_op jit(solution)/shard_map/pallas_call | solution.py:694
  159.5 9.8 %all-to-all-done = bf16[32,120,128]{2,1,0:T(8,128)(2,1)} async-done(((bf16[32,120,128]{2,1,0:T(8,128)(2,1)}), bf16[32,120,128]{2,1,0:T(8,128)(2,1)}, u32[]{:S(2)}, u32[]{:S(2)}) %all-to-all-start) | async-done | bytes 983072 | tf_op jit(solution)/shard_map/all_to_all | solution.py:644
  169.3 20.1 %shard_map.254 = (bf16[3840,128]{1,0:T(8,128)(2,1)S(1)}, bf16[3840,128]{1,0:T(8,128)(2,1)S(1)}, bf16[640,3072]{1,0:T(8,128)(2,1)}, bf16[640,3072]{1,0:T(8,128)(2...) custom-call(s32[1]{0:T(128)} %bitcast.me_ref, ...), custom_call_target="tpu_custom_call" | custom-call | flops 10000000000 | bytes 30000000 | tf_op jit(solution)/shard_map/pallas_call | solution.py:715
  194.0 3.6 %all-to-all-start.2 = ((bf16[32,120,128]{2,1,0:T(8,128)(2,1)}), bf16[32,120,128]{2,1,0:T(8,128)(2,1)S(1)}, u32[]{:S(2)}, u32[]{:S(2)}) async-start(bf16[32,120,128]{2,1,0:T(8,128)(2,1)} %bitcast.19), calls=%async_computation.2 | async-start | bytes 1966080 | tf_op jit(solution)/shard_map/all_to_all | solution.py:644
  203.3 14.3 %shard_map.257 = (f32[1,768,3072]{2,1,0:T(8,128)}, f32[1,3072,768]{2,1,0:T(8,128)}, f32[768,128]{1,0:T(8,128)S(1)}) custom-call(bf16[640,768]{1,0:T(8,128)(2,1)S(1)} %copy-done.71, bf16[640,768]{1,0:T(8,128)(2,1)S(1)} %copy-done.73, bf16[640,128]{1,0:T(8,128)(2,1)S(1)} %copy-done.77, bf16[768,768]{1,0:T(8,128)(2,1)S(1)} %copy-done.4, ...), custom_call_target="tpu_custom_call" | custom-call | flops 7000000000 | bytes 30000000 | tf_op jit(solution)/shard_map/pallas_call | solution.py:757
  217.6 4.8 %all-to-all-done.2 = bf16[32,120,128]{2,1,0:T(8,128)(2,1)S(1)} async-done(((bf16[32,120,128]{2,1,0:T(8,128)(2,1)}), bf16[32,120,128]{2,1,0:T(8,128)(2,1)S(1)}, u32[]{:S(2)}, u32[]{:S(2)}) %all-to-all-start.2) | async-done | bytes 983072 | tf_op jit(solution)/shard_map/all_to_all | solution.py:644
  224.7 6.5 %shard_map.258 = (f32[512,768]{1,0:T(8,128)}, bf16[512,768]{1,0:T(8,128)(2,1)S(1)}, f32[384,896]{1,0:T(8,128)}, bf16[384,896]{1,0:T(8,128)(2,1)S(1)}) custom-call(bf16[3840,128]{1,0:T(8,128)(2,1)S(1)} %bitcast.17, bf16[512,640]{1,0:T(8,128)(2,1)S(1)} %get-tuple-element.98.dt_ref, f32[512,768]{1,0:T(8,128)} %get-tuple-element.99.after_ref, ...), custom_call_target="tpu_custom_call" | custom-call | flops 2000000000 | bytes 10000000 | tf_op jit(solution)/shard_map/pallas_call | solution.py:780
  232.8 7.4 %shard_map.259 = (bf16[512,768]{1,0:T(8,128)(2,1)S(1)}, f32[384,768]{1,0:T(8,128)S(1)}, bf16[384,768]{1,0:T(8,128)(2,1)S(1)}, f32[8,512]{1,0:T(8,128)S(1)}) custom-call(bf16[512,768]{1,0:T(8,128)(2,1)S(1)} %copy-done.60, bf16[4,512,512]{2,1,0:T(8,128)(2,1)} %get-tuple-element.112.probs_ref, bf16[512,256]{1,0:T(8,128)(2,1)S(1)} %get-tuple-element.162.gm_ref, ...), custom_call_target="tpu_custom_call" | custom-call | flops 4000000000 | bytes 8000000 | tf_op jit(solution)/shard_map/pallas_call | solution.py:804
  241.0 8.0 %shard_map.260 = (bf16[512,768]{1,0:T(8,128)(2,1)S(1)}, f32[384,768]{1,0:T(8,128)S(1)}, bf16[384,768]{1,0:T(8,128)(2,1)}, f32[8,512]{1,0:T(8,128)S(1)}) custom-call(bf16[512,768]{1,0:T(8,128)(2,1)S(1)} %copy-done.64, bf16[4,512,512]{2,1,0:T(8,128)(2,1)} %copy-done.58, bf16[512,256]{1,0:T(8,128)(2,1)S(1)} %get-tuple-element.161.gm_ref, ...), custom_call_target="tpu_custom_call" | custom-call | flops 4000000000 | bytes 8000000 | tf_op jit(solution)/shard_map/pallas_call | solution.py:804
  251.0 7.8 %shard_map.261 = (bf16[512,768]{1,0:T(8,128)(2,1)S(1)}, f32[384,768]{1,0:T(8,128)S(1)}, bf16[384,768]{1,0:T(8,128)(2,1)S(1)}, f32[8,512]{1,0:T(8,128)S(1)}) custom-call(bf16[512,768]{1,0:T(8,128)(2,1)S(1)} %copy-done.62, bf16[4,512,512]{2,1,0:T(8,128)(2,1)} %copy-done.57, bf16[512,256]{1,0:T(8,128)(2,1)S(1)} %get-tuple-element.160.gm_ref, ...), custom_call_target="tpu_custom_call" | custom-call | flops 4000000000 | bytes 8000000 | tf_op jit(solution)/shard_map/pallas_call | solution.py:804
  261.6 7.9 %shard_map.262 = (bf16[512,768]{1,0:T(8,128)(2,1)}, f32[384,128]{1,0:T(8,128)S(1)}, bf16[384,128]{1,0:T(8,128)(2,1)S(1)}) custom-call(bf16[512,768]{1,0:T(8,128)(2,1)S(1)} %copy-done.54, f32[8,768]{1,0:T(8,128)S(1)} %get-tuple-element.101.gain_ref, bf16[768,768]{1,0:T(8,128)(2,1)} %get-tuple-element.84.perm_ref, f32[512,768]{1,0:T(8,128)} %get-tuple-element.110.after_ref, ...), custom_call_target="tpu_custom_call" | custom-call | flops 4000000000 | bytes 10000000 | tf_op jit(solution)/shard_map/pallas_call | solution.py:818
  270.9 1.5 collective-permute-start.29
  272.4 1.5 collective-permute-start.31
  274.8 2.3 collective-permute-done.31
  279.5 1.8 collective-permute-start.33
  281.3 2.9 all-to-all-start.3
  286.4 1.6 fusion.25
  288.1 1.7 collective-permute-start.50
  289.8 1.5 collective-permute-start.52
  291.8 1.7 collective-permute-start.57
  293.7 1.5 collective-permute-start.59
  295.5 3.1 collective-permute-done.50
  298.6 1.5 collective-permute-start.58
  300.1 3.4 collective-permute-done.52
  304.7 1.6 collective-permute-start.45
  306.7 1.8 collective-permute-start.44
  308.5 3.0 collective-permute-done.59
  315.4 2.5 collective-permute-done.45
  317.9 3.4 collective-permute-start.55
  322.4 1.5 collective-permute-done.55
  323.9 3.4 collective-permute-start.62
  329.8 3.3 collective-permute-start.48
  333.8 1.7 collective-permute-done.48
  335.6 2.4 collective-permute-done.47
  339.9 3.3 collective-permute-start.41
  343.9 1.9 collective-permute-done.41
  345.7 2.4 collective-permute-done.40
  352.2 2.3 shard_map.255
  (337 shorter events, 82.6 us)
Async XLA Ops:
  5.0 62.5 %collective-permute-start.2 = (bf16[24,896]{1,0:T(8,128)(2,1)S(1)}, bf16[24,896]{1,0:T(8,128)(2,1)S(1)}, u32[]{:S(2)}, u32[]{:S(2)}) collective-permute-start(bf16[24,896]{1,0:T(8,128)(2,1)S(1)} %concatenate.49), channel_id=1, source_target_pairs={{0,24},{1,25},{2,26},{3,27},{4,28},{5,29},{6,30},{7,31},{8,16},{9,... | collective-permute-start | bytes 129032 | tf_op jit(solution)/shard_map/ppermute | solution.py:44
  10.0 59.3 %collective-permute-start.1 = (bf16[24,896]{1,0:T(8,128)(2,1)S(1)}, bf16[24,896]{1,0:T(8,128)(2,1)S(1)}, u32[]{:S(2)}, u32[]{:S(2)}) collective-permute-start(bf16[24,896]{1,0:T(8,128)(2,1)S(1)} %concatenate.49), channel_id=1, source_target_pairs={{0,16},{1,17},{2,18},{3,19},{4,20},{5,21},{6,22},{7,23},{8,24},{9,... | collective-permute-start | bytes 129032 | tf_op jit(solution)/shard_map/ppermute | solution.py:44
  10.0 55.8 %collective-permute-start = (bf16[24,896]{1,0:T(8,128)(2,1)S(1)}, bf16[24,896]{1,0:T(8,128)(2,1)S(1)}, u32[]{:S(2)}, u32[]{:S(2)}) collective-permute-start(bf16[24,896]{1,0:T(8,128)(2,1)S(1)} %concatenate.49), channel_id=1, source_target_pairs={{0,8},{1,9},{2,10},{3,11},{4,12},{5,13},{6,14},{7,15},{8,0},{9,1},... | collective-permute-start | bytes 129032 | tf_op jit(solution)/shard_map/ppermute | solution.py:44
  11.3 23.0 %collective-permute-start.15 = (bf16[24,768]{1,0:T(8,128)(2,1)S(1)}, bf16[24,768]{1,0:T(8,128)(2,1)S(1)}, u32[]{:S(2)}, u32[]{:S(2)}) collective-permute-start(bf16[24,768]{1,0:T(8,128)(2,1)S(1)} %get-tuple-element.199), channel_id=1, source_target_pairs={{0,16},{1,17},{2,18},{3,19},{4,20},{5,21},{6,22},{7,23},{8,24},{9,... | collective-permute-start | bytes 110600 | tf_op jit(solution)/shard_map/ppermute | solution.py:44
  13.6 16.4 %collective-permute-start.14 = (bf16[24,768]{1,0:T(8,128)(2,1)S(1)}, bf16[24,768]{1,0:T(8,128)(2,1)S(1)}, u32[]{:S(2)}, u32[]{:S(2)}) collective-permute-start(bf16[24,768]{1,0:T(8,128)(2,1)S(1)} %get-tuple-element.199), channel_id=1, source_target_pairs={{0,8},{1,9},{2,10},{3,11},{4,12},{5,13},{6,14},{7,15},{8,0},{9,1},... | collective-permute-start | bytes 110600 | tf_op jit(solution)/shard_map/ppermute | solution.py:44
  26.7 110.7 %all-to-all-start.1 = ((bf16[32,120,128]{2,1,0:T(8,128)(2,1)}), bf16[32,120,128]{2,1,0:T(8,128)(2,1)S(1)}, u32[]{:S(2)}, u32[]{:S(2)}) async-start(bf16[32,120,128]{2,1,0:T(8,128)(2,1)} %bitcast.6), calls=%async_computation.1 | async-start | bytes 1966080 | tf_op jit(solution)/shard_map/all_to_all | solution.py:644
  30.0 21.3 %collective-permute-start.16 = (bf16[24,768]{1,0:T(8,128)(2,1)S(1)}, bf16[24,768]{1,0:T(8,128)(2,1)S(1)}, u32[]{:S(2)}, u32[]{:S(2)}) collective-permute-start(bf16[24,768]{1,0:T(8,128)(2,1)S(1)} %get-tuple-element.199), channel_id=1, source_target_pairs={{0,24},{1,25},{2,26},{3,27},{4,28},{5,29},{6,30},{7,31},{8,16},{9,... | collective-permute-start | bytes 110600 | tf_op jit(solution)/shard_map/ppermute | solution.py:44
  34.3 26.4 %collective-permute-start.8 = (bf16[24,768]{1,0:T(8,128)(2,1)S(1)}, bf16[24,768]{1,0:T(8,128)(2,1)S(1)}, u32[]{:S(2)}, u32[]{:S(2)}) collective-permute-start(bf16[24,768]{1,0:T(8,128)(2,1)S(1)} %get-tuple-element.210), channel_id=1, source_target_pairs={{0,16},{1,17},{2,18},{3,19},{4,20},{5,21},{6,22},{7,23},{8,24},{9,... | collective-permute-start | bytes 110600 | tf_op jit(solution)/shard_map/ppermute | solution.py:44
  51.3 8.4 %collective-permute-start.7 = (bf16[24,768]{1,0:T(8,128)(2,1)S(1)}, bf16[24,768]{1,0:T(8,128)(2,1)S(1)}, u32[]{:S(2)}, u32[]{:S(2)}) collective-permute-start(bf16[24,768]{1,0:T(8,128)(2,1)S(1)} %get-tuple-element.210), channel_id=1, source_target_pairs={{0,8},{1,9},{2,10},{3,11},{4,12},{5,13},{6,14},{7,15},{8,0},{9,1},... | collective-permute-start | bytes 110600 | tf_op jit(solution)/shard_map/ppermute | solution.py:44
  59.7 6.2 %collective-permute-start.9 = (bf16[24,768]{1,0:T(8,128)(2,1)S(1)}, bf16[24,768]{1,0:T(8,128)(2,1)S(1)}, u32[]{:S(2)}, u32[]{:S(2)}) collective-permute-start(bf16[24,768]{1,0:T(8,128)(2,1)S(1)} %get-tuple-element.210), channel_id=1, source_target_pairs={{0,24},{1,25},{2,26},{3,27},{4,28},{5,29},{6,30},{7,31},{8,16},{9,... | collective-permute-start | bytes 110600 | tf_op jit(solution)/shard_map/ppermute | solution.py:44
  60.8 10.5 %collective-permute-start.22 = (bf16[24,896]{1,0:T(8,128)(2,1)S(1)}, bf16[24,896]{1,0:T(8,128)(2,1)S(1)}, u32[]{:S(2)}, u32[]{:S(2)}) collective-permute-start(bf16[24,896]{1,0:T(8,128)(2,1)S(1)} %get-tuple-element.159), channel_id=1, source_target_pairs={{0,16},{1,17},{2,18},{3,19},{4,20},{5,21},{6,22},{7,23},{8,24},{9,... | collective-permute-start | bytes 129032 | tf_op jit(solution)/shard_map/ppermute | solution.py:44
  65.8 4.4 %collective-permute-start.21 = (bf16[24,896]{1,0:T(8,128)(2,1)S(1)}, bf16[24,896]{1,0:T(8,128)(2,1)S(1)}, u32[]{:S(2)}, u32[]{:S(2)}) collective-permute-start(bf16[24,896]{1,0:T(8,128)(2,1)S(1)} %get-tuple-element.159), channel_id=1, source_target_pairs={{0,8},{1,9},{2,10},{3,11},{4,12},{5,13},{6,14},{7,15},{8,0},{9,1},... | collective-permute-start | bytes 129032 | tf_op jit(solution)/shard_map/ppermute | solution.py:44
  65.9 6.8 %collective-permute-start.23 = (bf16[24,896]{1,0:T(8,128)(2,1)S(1)}, bf16[24,896]{1,0:T(8,128)(2,1)S(1)}, u32[]{:S(2)}, u32[]{:S(2)}) collective-permute-start(bf16[24,896]{1,0:T(8,128)(2,1)S(1)} %get-tuple-element.159), channel_id=1, source_target_pairs={{0,24},{1,25},{2,26},{3,27},{4,28},{5,29},{6,30},{7,31},{8,16},{9,... | collective-permute-start | bytes 129032 | tf_op jit(solution)/shard_map/ppermute | solution.py:44
  67.5 28.9 %collective-permute-start.19 = (bf16[96,768]{1,0:T(8,128)(2,1)S(1)}, bf16[96,768]{1,0:T(8,128)(2,1)S(1)}, u32[]{:S(2)}, u32[]{:S(2)}) collective-permute-start(bf16[96,768]{1,0:T(8,128)(2,1)S(1)} %pad_maximum_fusion.3), channel_id=1, source_target_pairs={{0,6},{1,7},{2,4},{3,5},{4,2},{5,3},{6,0},{7,1},{8,14},{9,15},{10,... | collective-permute-start | bytes 442376 | tf_op jit(solution)/shard_map/ppermute | solution.py:44
  69.3 25.8 %collective-permute-start.18 = (bf16[96,768]{1,0:T(8,128)(2,1)S(1)}, bf16[96,768]{1,0:T(8,128)(2,1)S(1)}, u32[]{:S(2)}, u32[]{:S(2)}) collective-permute-start(bf16[96,768]{1,0:T(8,128)(2,1)S(1)} %pad_maximum_fusion.3), channel_id=1, source_target_pairs={{0,4},{1,5},{2,6},{3,7},{4,0},{5,1},{6,2},{7,3},{8,12},{9,13},{10,... | collective-permute-start | bytes 442376 | tf_op jit(solution)/shard_map/ppermute | solution.py:44
  70.3 24.2 %collective-permute-start.17 = (bf16[96,768]{1,0:T(8,128)(2,1)S(1)}, bf16[96,768]{1,0:T(8,128)(2,1)S(1)}, u32[]{:S(2)}, u32[]{:S(2)}) collective-permute-start(bf16[96,768]{1,0:T(8,128)(2,1)S(1)} %pad_maximum_fusion.3), channel_id=1, source_target_pairs={{0,2},{1,3},{2,0},{3,1},{4,6},{5,7},{6,4},{7,5},{8,10},{9,11},{10,... | collective-permute-start | bytes 442376 | tf_op jit(solution)/shard_map/ppermute | solution.py:44
  71.3 8.6 %collective-permute-start.4 = (bf16[96,896]{1,0:T(8,128)(2,1)S(1)}, bf16[96,896]{1,0:T(8,128)(2,1)S(1)}, u32[]{:S(2)}, u32[]{:S(2)}) collective-permute-start(bf16[96,896]{1,0:T(8,128)(2,1)S(1)} %pad_maximum_fusion), channel_id=1, source_target_pairs={{0,4},{1,5},{2,6},{3,7},{4,0},{5,1},{6,2},{7,3},{8,12},{9,13},{10,... | collective-permute-start | bytes 516104 | tf_op jit(solution)/shard_map/ppermute | solution.py:44
  72.6 5.7 %collective-permute-start.3 = (bf16[96,896]{1,0:T(8,128)(2,1)S(1)}, bf16[96,896]{1,0:T(8,128)(2,1)S(1)}, u32[]{:S(2)}, u32[]{:S(2)}) collective-permute-start(bf16[96,896]{1,0:T(8,128)(2,1)S(1)} %pad_maximum_fusion), channel_id=1, source_target_pairs={{0,2},{1,3},{2,0},{3,1},{4,6},{5,7},{6,4},{7,5},{8,10},{9,11},{10,... | collective-permute-start | bytes 516104 | tf_op jit(solution)/shard_map/ppermute | solution.py:44
  78.3 6.4 %collective-permute-start.5 = (bf16[96,896]{1,0:T(8,128)(2,1)S(1)}, bf16[96,896]{1,0:T(8,128)(2,1)S(1)}, u32[]{:S(2)}, u32[]{:S(2)}) collective-permute-start(bf16[96,896]{1,0:T(8,128)(2,1)S(1)} %pad_maximum_fusion), channel_id=1, source_target_pairs={{0,6},{1,7},{2,4},{3,5},{4,2},{5,3},{6,0},{7,1},{8,14},{9,15},{10,... | collective-permute-start | bytes 516104 | tf_op jit(solution)/shard_map/ppermute | solution.py:44
  79.9 7.5 %collective-permute-start.24 = (bf16[96,896]{1,0:T(8,128)(2,1)S(1)}, bf16[96,896]{1,0:T(8,128)(2,1)S(1)}, u32[]{:S(2)}, u32[]{:S(2)}) collective-permute-start(bf16[96,896]{1,0:T(8,128)(2,1)S(1)} %pad_maximum_fusion.1), channel_id=1, source_target_pairs={{0,2},{1,3},{2,0},{3,1},{4,6},{5,7},{6,4},{7,5},{8,10},{9,11},{10,... | collective-permute-start | bytes 516104 | tf_op jit(solution)/shard_map/ppermute | solution.py:44
  84.7 5.4 %collective-permute-start.25 = (bf16[96,896]{1,0:T(8,128)(2,1)S(1)}, bf16[96,896]{1,0:T(8,128)(2,1)S(1)}, u32[]{:S(2)}, u32[]{:S(2)}) collective-permute-start(bf16[96,896]{1,0:T(8,128)(2,1)S(1)} %pad_maximum_fusion.1), channel_id=1, source_target_pairs={{0,4},{1,5},{2,6},{3,7},{4,0},{5,1},{6,2},{7,3},{8,12},{9,13},{10,... | collective-permute-start | bytes 516104 | tf_op jit(solution)/shard_map/ppermute | solution.py:44
  87.5 7.0 %collective-permute-start.26 = (bf16[96,896]{1,0:T(8,128)(2,1)S(1)}, bf16[96,896]{1,0:T(8,128)(2,1)S(1)}, u32[]{:S(2)}, u32[]{:S(2)}) collective-permute-start(bf16[96,896]{1,0:T(8,128)(2,1)S(1)} %pad_maximum_fusion.1), channel_id=1, source_target_pairs={{0,6},{1,7},{2,4},{3,5},{4,2},{5,3},{6,0},{7,1},{8,14},{9,15},{10,... | collective-permute-start | bytes 516104 | tf_op jit(solution)/shard_map/ppermute | solution.py:44
  90.1 11.8 %collective-permute-start.12 = (bf16[96,768]{1,0:T(8,128)(2,1)S(1)}, bf16[96,768]{1,0:T(8,128)(2,1)S(1)}, u32[]{:S(2)}, u32[]{:S(2)}) collective-permute-start(bf16[96,768]{1,0:T(8,128)(2,1)S(1)} %pad_maximum_fusion.2), channel_id=1, source_target_pairs={{0,6},{1,7},{2,4},{3,5},{4,2},{5,3},{6,0},{7,1},{8,14},{9,15},{10,... | collective-permute-start | bytes 442376 | tf_op jit(solution)/shard_map/ppermute | solution.py:44
  94.5 9.4 %collective-permute-start.6 = (bf16[384,896]{1,0:T(8,128)(2,1)S(1)}, bf16[384,896]{1,0:T(8,128)(2,1)S(1)}, u32[]{:S(2)}, u32[]{:S(2)}) collective-permute-start(bf16[384,896]{1,0:T(8,128)(2,1)S(1)} %constant_dynamic-update-slice_fusion.refs_1_.own0), channel_id=1, source_target_pairs={{0,1},{1,0},{2,3},{3,2},{4,5},{5,4},{6,7},{7,6},{8,9},{9,8},{10,11... | collective-permute-start | bytes 2064392 | tf_op jit(solution)/shard_map/ppermute | solution.py:44
  94.5 7.6 %collective-permute-start.27 = (bf16[384,896]{1,0:T(8,128)(2,1)S(1)}, bf16[384,896]{1,0:T(8,128)(2,1)S(1)}, u32[]{:S(2)}, u32[]{:S(2)}) collective-permute-start(bf16[384,896]{1,0:T(8,128)(2,1)S(1)} %constant_dynamic-update-slice_fusion.21.own_ref), channel_id=1, source_target_pairs={{0,1},{1,0},{2,3},{3,2},{4,5},{5,4},{6,7},{7,6},{8,9},{9,8},{10,11... | collective-permute-start | bytes 2064392 | tf_op jit(solution)/shard_map/ppermute | solution.py:44
  95.1 5.8 %collective-permute-start.10 = (bf16[96,768]{1,0:T(8,128)(2,1)S(1)}, bf16[96,768]{1,0:T(8,128)(2,1)S(1)}, u32[]{:S(2)}, u32[]{:S(2)}) collective-permute-start(bf16[96,768]{1,0:T(8,128)(2,1)S(1)} %pad_maximum_fusion.2), channel_id=1, source_target_pairs={{0,2},{1,3},{2,0},{3,1},{4,6},{5,7},{6,4},{7,5},{8,10},{9,11},{10,... | collective-permute-start | bytes 442376 | tf_op jit(solution)/shard_map/ppermute | solution.py:44
  96.4 5.6 %collective-permute-start.11 = (bf16[96,768]{1,0:T(8,128)(2,1)S(1)}, bf16[96,768]{1,0:T(8,128)(2,1)S(1)}, u32[]{:S(2)}, u32[]{:S(2)}) collective-permute-start(bf16[96,768]{1,0:T(8,128)(2,1)S(1)} %pad_maximum_fusion.2), channel_id=1, source_target_pairs={{0,4},{1,5},{2,6},{3,7},{4,0},{5,1},{6,2},{7,3},{8,12},{9,13},{10,... | collective-permute-start | bytes 442376 | tf_op jit(solution)/shard_map/ppermute | solution.py:44
  100.9 12.3 %collective-permute-start.20 = (bf16[384,768]{1,0:T(8,128)(2,1)S(1)}, bf16[384,768]{1,0:T(8,128)(2,1)S(1)}, u32[]{:S(2)}, u32[]{:S(2)}) collective-permute-start(bf16[384,768]{1,0:T(8,128)(2,1)S(1)} %constant_dynamic-update-slice_fusion.14.refs_2_.own2), channel_id=1, source_target_pairs={{0,1},{1,0},{2,3},{3,2},{4,5},{5,4},{6,7},{7,6},{8,9},{9,8},{10,11... | collective-permute-start | bytes 1769480 | tf_op jit(solution)/shard_map/ppermute | solution.py:44
  102.0 20.7 %collective-permute-start.13 = (bf16[384,768]{1,0:T(8,128)(2,1)S(1)}, bf16[384,768]{1,0:T(8,128)(2,1)S(1)}, u32[]{:S(2)}, u32[]{:S(2)}) collective-permute-start(bf16[384,768]{1,0:T(8,128)(2,1)S(1)} %constant_dynamic-update-slice_fusion.7.refs_2_.own1), channel_id=1, source_target_pairs={{0,1},{1,0},{2,3},{3,2},{4,5},{5,4},{6,7},{7,6},{8,9},{9,8},{10,11... | collective-permute-start | bytes 1769480 | tf_op jit(solution)/shard_map/ppermute | solution.py:44
  137.4 31.9 %all-to-all-start = ((bf16[32,120,128]{2,1,0:T(8,128)(2,1)}), bf16[32,120,128]{2,1,0:T(8,128)(2,1)}, u32[]{:S(2)}, u32[]{:S(2)}) async-start(bf16[32,120,128]{2,1,0:T(8,128)(2,1)} %bitcast.20), calls=%async_computation | async-start | bytes 1966080 | tf_op jit(solution)/shard_map/all_to_all | solution.py:644
  194.0 28.5 %all-to-all-start.2 = ((bf16[32,120,128]{2,1,0:T(8,128)(2,1)}), bf16[32,120,128]{2,1,0:T(8,128)(2,1)S(1)}, u32[]{:S(2)}, u32[]{:S(2)}) async-start(bf16[32,120,128]{2,1,0:T(8,128)(2,1)} %bitcast.19), calls=%async_computation.2 | async-start | bytes 1966080 | tf_op jit(solution)/shard_map/all_to_all | solution.py:644
  272.4 4.7 %collective-permute-start.31 = (bf16[96,128]{1,0:T(8,128)(2,1)S(1)}, bf16[96,128]{1,0:T(8,128)(2,1)S(1)}, u32[]{:S(2)}, u32[]{:S(2)}) collective-permute-start(bf16[96,128]{1,0:T(8,128)(2,1)S(1)} %get-tuple-element.188), channel_id=1, source_target_pairs={{0,6},{1,7},{2,4},{3,5},{4,2},{5,3},{6,0},{7,1},{8,14},{9,15},{10,... | collective-permute-start | bytes 73736 | tf_op jit(solution)/shard_map/ppermute | solution.py:44
  274.5 11.9 %collective-permute-start.49 = (bf16[384,768]{1,0:T(8,128)(2,1)}, bf16[384,768]{1,0:T(8,128)(2,1)}, u32[]{:S(2)}, u32[]{:S(2)}) collective-permute-start(bf16[384,768]{1,0:T(8,128)(2,1)} %get-tuple-element.133), channel_id=1, source_target_pairs={{0,1},{1,0},{2,3},{3,2},{4,5},{5,4},{6,7},{7,6},{8,9},{9,8},{10,11... | collective-permute-start | bytes 1769480 | tf_op jit(solution)/shard_map/ppermute | solution.py:44
  277.8 6.8 %collective-permute-start.32 = (bf16[24,128]{1,0:T(8,128)(2,1)S(1)}, bf16[24,128]{1,0:T(8,128)(2,1)S(1)}, u32[]{:S(2)}, u32[]{:S(2)}) collective-permute-start(bf16[24,128]{1,0:T(8,128)(2,1)S(1)} %get-tuple-element.212), channel_id=1, source_target_pairs={{0,8},{1,9},{2,10},{3,11},{4,12},{5,13},{6,14},{7,15},{8,0},{9,1},... | collective-permute-start | bytes 18440 | tf_op jit(solution)/shard_map/ppermute | solution.py:44
  278.4 6.4 %collective-permute-start.34 = (bf16[24,128]{1,0:T(8,128)(2,1)S(1)}, bf16[24,128]{1,0:T(8,128)(2,1)S(1)}, u32[]{:S(2)}, u32[]{:S(2)}) collective-permute-start(bf16[24,128]{1,0:T(8,128)(2,1)S(1)} %get-tuple-element.213), channel_id=1, source_target_pairs={{0,24},{1,25},{2,26},{3,27},{4,28},{5,29},{6,30},{7,31},{8,16},{9,... | collective-permute-start | bytes 18440 | tf_op jit(solution)/shard_map/ppermute | solution.py:44
  279.5 5.5 %collective-permute-start.33 = (bf16[24,128]{1,0:T(8,128)(2,1)S(1)}, bf16[24,128]{1,0:T(8,128)(2,1)S(1)}, u32[]{:S(2)}, u32[]{:S(2)}) collective-permute-start(bf16[24,128]{1,0:T(8,128)(2,1)S(1)} %get-tuple-element.214), channel_id=1, source_target_pairs={{0,16},{1,17},{2,18},{3,19},{4,20},{5,21},{6,22},{7,23},{8,24},{9,... | collective-permute-start | bytes 18440 | tf_op jit(solution)/shard_map/ppermute | solution.py:44
  281.3 68.8 %all-to-all-start.3 = ((bf16[32,120,128]{2,1,0:T(8,128)(2,1)}), bf16[32,120,128]{2,1,0:T(8,128)(2,1)S(1)}, u32[]{:S(2)}, u32[]{:S(2)}) async-start(bf16[32,120,128]{2,1,0:T(8,128)(2,1)} %bitcast.18), calls=%async_computation.3 | async-start | bytes 1966080 | tf_op jit(solution)/shard_map/all_to_all | solution.py:644
  284.2 9.5 %collective-permute-start.35 = (bf16[384,896]{1,0:T(8,128)(2,1)}, bf16[384,896]{1,0:T(8,128)(2,1)S(1)}, u32[]{:S(2)}, u32[]{:S(2)}) collective-permute-start(bf16[384,896]{1,0:T(8,128)(2,1)} %copy-done.27), channel_id=1, source_target_pairs={{0,1},{1,0},{2,3},{3,2},{4,5},{5,4},{6,7},{7,6},{8,9},{9,8},{10,11... | collective-permute-start | bytes 2064392 | tf_op jit(solution)/shard_map/ppermute | solution.py:44
  284.5 6.7 %collective-permute-start.56 = (bf16[384,768]{1,0:T(8,128)(2,1)}, bf16[384,768]{1,0:T(8,128)(2,1)S(1)}, u32[]{:S(2)}, u32[]{:S(2)}) collective-permute-start(bf16[384,768]{1,0:T(8,128)(2,1)} %copy-done.35), channel_id=1, source_target_pairs={{0,1},{1,0},{2,3},{3,2},{4,5},{5,4},{6,7},{7,6},{8,9},{9,8},{10,11... | collective-permute-start | bytes 1769480 | tf_op jit(solution)/shard_map/ppermute | solution.py:44
  284.8 7.0 %collective-permute-start.42 = (bf16[384,768]{1,0:T(8,128)(2,1)}, bf16[384,768]{1,0:T(8,128)(2,1)S(1)}, u32[]{:S(2)}, u32[]{:S(2)}) collective-permute-start(bf16[384,768]{1,0:T(8,128)(2,1)} %copy-done.30), channel_id=1, source_target_pairs={{0,1},{1,0},{2,3},{3,2},{4,5},{5,4},{6,7},{7,6},{8,9},{9,8},{10,11... | collective-permute-start | bytes 1769480 | tf_op jit(solution)/shard_map/ppermute | solution.py:44
  288.1 10.6 %collective-permute-start.50 = (bf16[96,768]{1,0:T(8,128)(2,1)S(1)}, bf16[96,768]{1,0:T(8,128)(2,1)S(1)}, u32[]{:S(2)}, u32[]{:S(2)}) collective-permute-start(bf16[96,768]{1,0:T(8,128)(2,1)S(1)} %get-tuple-element.169), channel_id=1, source_target_pairs={{0,2},{1,3},{2,0},{3,1},{4,6},{5,7},{6,4},{7,5},{8,10},{9,11},{10,... | collective-permute-start | bytes 442376 | tf_op jit(solution)/shard_map/ppermute | solution.py:44
  289.8 13.7 %collective-permute-start.52 = (bf16[96,768]{1,0:T(8,128)(2,1)S(1)}, bf16[96,768]{1,0:T(8,128)(2,1)S(1)}, u32[]{:S(2)}, u32[]{:S(2)}) collective-permute-start(bf16[96,768]{1,0:T(8,128)(2,1)S(1)} %get-tuple-element.170), channel_id=1, source_target_pairs={{0,6},{1,7},{2,4},{3,5},{4,2},{5,3},{6,0},{7,1},{8,14},{9,15},{10,... | collective-permute-start | bytes 442376 | tf_op jit(solution)/shard_map/ppermute | solution.py:44
  291.3 13.5 %collective-permute-start.51 = (bf16[96,768]{1,0:T(8,128)(2,1)S(1)}, bf16[96,768]{1,0:T(8,128)(2,1)S(1)}, u32[]{:S(2)}, u32[]{:S(2)}) collective-permute-start(bf16[96,768]{1,0:T(8,128)(2,1)S(1)} %get-tuple-element.171), channel_id=1, source_target_pairs={{0,4},{1,5},{2,6},{3,7},{4,0},{5,1},{6,2},{7,3},{8,12},{9,13},{10,... | collective-permute-start | bytes 442376 | tf_op jit(solution)/shard_map/ppermute | solution.py:44
  291.8 14.9 %collective-permute-start.57 = (bf16[96,768]{1,0:T(8,128)(2,1)S(1)}, bf16[96,768]{1,0:T(8,128)(2,1)S(1)}, u32[]{:S(2)}, u32[]{:S(2)}) collective-permute-start(bf16[96,768]{1,0:T(8,128)(2,1)S(1)} %get-tuple-element.172), channel_id=1, source_target_pairs={{0,2},{1,3},{2,0},{3,1},{4,6},{5,7},{6,4},{7,5},{8,10},{9,11},{10,... | collective-permute-start | bytes 442376 | tf_op jit(solution)/shard_map/ppermute | solution.py:44
  293.7 17.8 %collective-permute-start.59 = (bf16[96,768]{1,0:T(8,128)(2,1)S(1)}, bf16[96,768]{1,0:T(8,128)(2,1)S(1)}, u32[]{:S(2)}, u32[]{:S(2)}) collective-permute-start(bf16[96,768]{1,0:T(8,128)(2,1)S(1)} %get-tuple-element.173), channel_id=1, source_target_pairs={{0,6},{1,7},{2,4},{3,5},{4,2},{5,3},{6,0},{7,1},{8,14},{9,15},{10,... | collective-permute-start | bytes 442376 | tf_op jit(solution)/shard_map/ppermute | solution.py:44
  298.6 13.9 %collective-permute-start.58 = (bf16[96,768]{1,0:T(8,128)(2,1)S(1)}, bf16[96,768]{1,0:T(8,128)(2,1)S(1)}, u32[]{:S(2)}, u32[]{:S(2)}) collective-permute-start(bf16[96,768]{1,0:T(8,128)(2,1)S(1)} %get-tuple-element.174), channel_id=1, source_target_pairs={{0,4},{1,5},{2,6},{3,7},{4,0},{5,1},{6,2},{7,3},{8,12},{9,13},{10,... | collective-permute-start | bytes 442376 | tf_op jit(solution)/shard_map/ppermute | solution.py:44
  303.5 10.5 %collective-permute-start.43 = (bf16[96,768]{1,0:T(8,128)(2,1)S(1)}, bf16[96,768]{1,0:T(8,128)(2,1)S(1)}, u32[]{:S(2)}, u32[]{:S(2)}) collective-permute-start(bf16[96,768]{1,0:T(8,128)(2,1)S(1)} %get-tuple-element.166), channel_id=1, source_target_pairs={{0,2},{1,3},{2,0},{3,1},{4,6},{5,7},{6,4},{7,5},{8,10},{9,11},{10,... | collective-permute-start | bytes 442376 | tf_op jit(solution)/shard_map/ppermute | solution.py:44
  304.7 13.1 %collective-permute-start.45 = (bf16[96,768]{1,0:T(8,128)(2,1)S(1)}, bf16[96,768]{1,0:T(8,128)(2,1)S(1)}, u32[]{:S(2)}, u32[]{:S(2)}) collective-permute-start(bf16[96,768]{1,0:T(8,128)(2,1)S(1)} %get-tuple-element.167), channel_id=1, source_target_pairs={{0,6},{1,7},{2,4},{3,5},{4,2},{5,3},{6,0},{7,1},{8,14},{9,15},{10,... | collective-permute-start | bytes 442376 | tf_op jit(solution)/shard_map/ppermute | solution.py:44
  306.7 14.6 %collective-permute-start.44 = (bf16[96,768]{1,0:T(8,128)(2,1)S(1)}, bf16[96,768]{1,0:T(8,128)(2,1)S(1)}, u32[]{:S(2)}, u32[]{:S(2)}) collective-permute-start(bf16[96,768]{1,0:T(8,128)(2,1)S(1)} %get-tuple-element.168), channel_id=1, source_target_pairs={{0,4},{1,5},{2,6},{3,7},{4,0},{5,1},{6,2},{7,3},{8,12},{9,13},{10,... | collective-permute-start | bytes 442376 | tf_op jit(solution)/shard_map/ppermute | solution.py:44
  311.5 27.8 %collective-permute-start.36 = (bf16[96,896]{1,0:T(8,128)(2,1)S(1)}, bf16[96,896]{1,0:T(8,128)(2,1)S(1)}, u32[]{:S(2)}, u32[]{:S(2)}) collective-permute-start(bf16[96,896]{1,0:T(8,128)(2,1)S(1)} %get-tuple-element.163), channel_id=1, source_target_pairs={{0,2},{1,3},{2,0},{3,1},{4,6},{5,7},{6,4},{7,5},{8,10},{9,11},{10,... | collective-permute-start | bytes 516104 | tf_op jit(solution)/shard_map/ppermute | solution.py:44
  312.5 26.8 %collective-permute-start.38 = (bf16[96,896]{1,0:T(8,128)(2,1)S(1)}, bf16[96,896]{1,0:T(8,128)(2,1)S(1)}, u32[]{:S(2)}, u32[]{:S(2)}) collective-permute-start(bf16[96,896]{1,0:T(8,128)(2,1)S(1)} %get-tuple-element.164), channel_id=1, source_target_pairs={{0,6},{1,7},{2,4},{3,5},{4,2},{5,3},{6,0},{7,1},{8,14},{9,15},{10,... | collective-permute-start | bytes 516104 | tf_op jit(solution)/shard_map/ppermute | solution.py:44
  314.0 7.5 %collective-permute-start.53 = (bf16[24,768]{1,0:T(8,128)(2,1)S(1)}, bf16[24,768]{1,0:T(8,128)(2,1)S(1)}, u32[]{:S(2)}, u32[]{:S(2)}) collective-permute-start(bf16[24,768]{1,0:T(8,128)(2,1)S(1)} %get-tuple-element.181), channel_id=1, source_target_pairs={{0,8},{1,9},{2,10},{3,11},{4,12},{5,13},{6,14},{7,15},{8,0},{9,1},... | collective-permute-start | bytes 110600 | tf_op jit(solution)/shard_map/ppermute | solution.py:44
  317.9 6.1 %collective-permute-start.55 = (bf16[24,768]{1,0:T(8,128)(2,1)S(1)}, bf16[24,768]{1,0:T(8,128)(2,1)S(1)}, u32[]{:S(2)}, u32[]{:S(2)}) collective-permute-start(bf16[24,768]{1,0:T(8,128)(2,1)S(1)} %get-tuple-element.182), channel_id=1, source_target_pairs={{0,24},{1,25},{2,26},{3,27},{4,28},{5,29},{6,30},{7,31},{8,16},{9,... | collective-permute-start | bytes 110600 | tf_op jit(solution)/shard_map/ppermute | solution.py:44
  321.3 6.0 %collective-permute-start.54 = (bf16[24,768]{1,0:T(8,128)(2,1)S(1)}, bf16[24,768]{1,0:T(8,128)(2,1)S(1)}, u32[]{:S(2)}, u32[]{:S(2)}) collective-permute-start(bf16[24,768]{1,0:T(8,128)(2,1)S(1)} %get-tuple-element.183), channel_id=1, source_target_pairs={{0,16},{1,17},{2,18},{3,19},{4,20},{5,21},{6,22},{7,23},{8,24},{9,... | collective-permute-start | bytes 110600 | tf_op jit(solution)/shard_map/ppermute | solution.py:44
  321.5 5.9 %collective-permute-start.60 = (bf16[24,768]{1,0:T(8,128)(2,1)S(1)}, bf16[24,768]{1,0:T(8,128)(2,1)S(1)}, u32[]{:S(2)}, u32[]{:S(2)}) collective-permute-start(bf16[24,768]{1,0:T(8,128)(2,1)S(1)} %get-tuple-element.184), channel_id=1, source_target_pairs={{0,8},{1,9},{2,10},{3,11},{4,12},{5,13},{6,14},{7,15},{8,0},{9,1},... | collective-permute-start | bytes 110600 | tf_op jit(solution)/shard_map/ppermute | solution.py:44
  323.9 5.9 %collective-permute-start.62 = (bf16[24,768]{1,0:T(8,128)(2,1)S(1)}, bf16[24,768]{1,0:T(8,128)(2,1)S(1)}, u32[]{:S(2)}, u32[]{:S(2)}) collective-permute-start(bf16[24,768]{1,0:T(8,128)(2,1)S(1)} %get-tuple-element.185), channel_id=1, source_target_pairs={{0,24},{1,25},{2,26},{3,27},{4,28},{5,29},{6,30},{7,31},{8,16},{9,... | collective-permute-start | bytes 110600 | tf_op jit(solution)/shard_map/ppermute | solution.py:44
  327.3 5.8 %collective-permute-start.61 = (bf16[24,768]{1,0:T(8,128)(2,1)S(1)}, bf16[24,768]{1,0:T(8,128)(2,1)S(1)}, u32[]{:S(2)}, u32[]{:S(2)}) collective-permute-start(bf16[24,768]{1,0:T(8,128)(2,1)S(1)} %get-tuple-element.186), channel_id=1, source_target_pairs={{0,16},{1,17},{2,18},{3,19},{4,20},{5,21},{6,22},{7,23},{8,24},{9,... | collective-permute-start | bytes 110600 | tf_op jit(solution)/shard_map/ppermute | solution.py:44
  327.4 5.8 %collective-permute-start.46 = (bf16[24,768]{1,0:T(8,128)(2,1)S(1)}, bf16[24,768]{1,0:T(8,128)(2,1)S(1)}, u32[]{:S(2)}, u32[]{:S(2)}) collective-permute-start(bf16[24,768]{1,0:T(8,128)(2,1)S(1)} %get-tuple-element.178), channel_id=1, source_target_pairs={{0,8},{1,9},{2,10},{3,11},{4,12},{5,13},{6,14},{7,15},{8,0},{9,1},... | collective-permute-start | bytes 110600 | tf_op jit(solution)/shard_map/ppermute | solution.py:44
  329.8 5.8 %collective-permute-start.48 = (bf16[24,768]{1,0:T(8,128)(2,1)S(1)}, bf16[24,768]{1,0:T(8,128)(2,1)S(1)}, u32[]{:S(2)}, u32[]{:S(2)}) collective-permute-start(bf16[24,768]{1,0:T(8,128)(2,1)S(1)} %get-tuple-element.179), channel_id=1, source_target_pairs={{0,24},{1,25},{2,26},{3,27},{4,28},{5,29},{6,30},{7,31},{8,16},{9,... | collective-permute-start | bytes 110600 | tf_op jit(solution)/shard_map/ppermute | solution.py:44
  333.1 4.9 %collective-permute-start.47 = (bf16[24,768]{1,0:T(8,128)(2,1)S(1)}, bf16[24,768]{1,0:T(8,128)(2,1)S(1)}, u32[]{:S(2)}, u32[]{:S(2)}) collective-permute-start(bf16[24,768]{1,0:T(8,128)(2,1)S(1)} %get-tuple-element.180), channel_id=1, source_target_pairs={{0,16},{1,17},{2,18},{3,19},{4,20},{5,21},{6,22},{7,23},{8,24},{9,... | collective-permute-start | bytes 110600 | tf_op jit(solution)/shard_map/ppermute | solution.py:44
  333.2 6.1 %collective-permute-start.37 = (bf16[96,896]{1,0:T(8,128)(2,1)S(1)}, bf16[96,896]{1,0:T(8,128)(2,1)S(1)}, u32[]{:S(2)}, u32[]{:S(2)}) collective-permute-start(bf16[96,896]{1,0:T(8,128)(2,1)S(1)} %get-tuple-element.165), channel_id=1, source_target_pairs={{0,4},{1,5},{2,6},{3,7},{4,0},{5,1},{6,2},{7,3},{8,12},{9,13},{10,... | collective-permute-start | bytes 516104 | tf_op jit(solution)/shard_map/ppermute | solution.py:44
  339.4 4.4 %collective-permute-start.39 = (bf16[24,896]{1,0:T(8,128)(2,1)S(1)}, bf16[24,896]{1,0:T(8,128)(2,1)S(1)}, u32[]{:S(2)}, u32[]{:S(2)}) collective-permute-start(bf16[24,896]{1,0:T(8,128)(2,1)S(1)} %get-tuple-element.175), channel_id=1, source_target_pairs={{0,8},{1,9},{2,10},{3,11},{4,12},{5,13},{6,14},{7,15},{8,0},{9,1},... | collective-permute-start | bytes 129032 | tf_op jit(solution)/shard_map/ppermute | solution.py:44
  339.9 5.8 %collective-permute-start.41 = (bf16[24,896]{1,0:T(8,128)(2,1)S(1)}, bf16[24,896]{1,0:T(8,128)(2,1)S(1)}, u32[]{:S(2)}, u32[]{:S(2)}) collective-permute-start(bf16[24,896]{1,0:T(8,128)(2,1)S(1)} %get-tuple-element.176), channel_id=1, source_target_pairs={{0,24},{1,25},{2,26},{3,27},{4,28},{5,29},{6,30},{7,31},{8,16},{9,... | collective-permute-start | bytes 129032 | tf_op jit(solution)/shard_map/ppermute | solution.py:44
  343.2 4.9 %collective-permute-start.40 = (bf16[24,896]{1,0:T(8,128)(2,1)S(1)}, bf16[24,896]{1,0:T(8,128)(2,1)S(1)}, u32[]{:S(2)}, u32[]{:S(2)}) collective-permute-start(bf16[24,896]{1,0:T(8,128)(2,1)S(1)} %get-tuple-element.177), channel_id=1, source_target_pairs={{0,16},{1,17},{2,18},{3,19},{4,20},{5,21},{6,22},{7,23},{8,24},{9,... | collective-permute-start | bytes 129032 | tf_op jit(solution)/shard_map/ppermute | solution.py:44
  (85 other events, 553.5 us)
